TPU v7x, 32 devices: a whole 2x2x4 slice. The times are simulated.
32 devices in a mesh: dp: 8 (over z, x), mp: 4 (over y, core).
Axes of the slice: x: 2, y: 2, z: 4, core: 2. Of those that a mesh axis runs over, the one named last changes fastest.
Arguments:
- tokens: bfloat16 [32768, 768], P(('dp', 'mp')), may hold values from -6 to 6
- segments: int32 [64, 512], P(('dp', 'mp')), may hold values from 0 to 5, never falling along the last dimension, each value on 1 to 256 neighbouring positions
- head_mask: int32 [12], replicated, may hold values 0 or 1
- unit_mask: int32 [3072], replicated, may hold values 0 or 1
- hidden_mask: int32 [768], replicated, may hold values 0 or 1
- layer_gates: float32 [2], replicated, may hold values from 0.5 to 1.5
- qkv_weight: bfloat16 [768, 2304], P('mp'), may hold values from -0.21875 to 0.21875
- out_weight: bfloat16 [768, 768], P('mp'), may hold values from -1.75 to 1.75
- norm_gain: float32 [768], replicated, may hold values from 0.5 to 1.5
- norm_bias: float32 [768], replicated, may hold values from -3 to 3
- up_weight: bfloat16 [768, 3072], P(None, 'mp'), may hold values from -0.21875 to 0.21875
- down_weight: bfloat16 [768, 3072], P(None, 'mp'), may hold values from -0.109375 to 0.109375
- cotangent: bfloat16 [32768, 768], P(('dp', 'mp')), may hold values from -6 to 6
- owner_slot: int32 [48], replicated, may hold values from 0 to 47, as said below
- master: float32 [48, 384, 384], P('dp', 'mp'), may hold values from -0.21875 to 0.21875
- left_stats: float32 [48, 384, 384], P('dp', 'mp'), may hold values from -12582912 to 50331648
- right_stats: float32 [48, 384, 384], P('dp', 'mp'), may hold values from -12582912 to 50331648
- left_root: float32 [48, 384, 384], P('dp', 'mp'), may hold values from -1 to 1
- right_root: float32 [48, 384, 384], P('dp'), may hold values from -1 to 1
Outputs:
- output: bfloat16 [32768, 768], P(('dp', 'mp'))
- input_grad: float32 [32768, 768], P(('dp', 'mp'))
- head_grad: float32 [12], replicated
- unit_grad: float32 [3072], replicated
- hidden_grad: float32 [768], replicated
- layer_grad: float32 [2], replicated
- norm_grad: float32 [2, 768], replicated
- norm_new: float32 [2, 768], replicated
- block_grad: float32 [48, 384, 384], P('dp', 'mp')
- left_new: float32 [48, 384, 384], P('dp', 'mp')
- right_new: float32 [48, 384, 384], P('dp', 'mp')
- weight_new: float32 [48, 384, 384], P('dp', 'mp')
- weight_copy: bfloat16 [48, 384, 384], P('dp', 'mp')
Inputs may be any that keep to these rules, and one draw needn't show every extreme that they name: `segments`: in every block of 512 positions the item numbers run from 0 to 5 and never fall; each item has 1 to 256 positions, and one item of each block has exactly 256. `owner_slot`: every slot number appears exactly once.
All inputs are finite; a program needn't handle non-finite values.
Results may differ from a plain program's by a relative error of at most 0.017.
Values may be sent and summed in bfloat16 or wider, within the bound.
A program may use at most 192 MiB of HBM per device.

v0:
```python
from functools import partial
import math

import jax
import jax.numpy as jnp
from jax import lax
from jax.sharding import PartitionSpec as P

FF = 3072
SB = 384


HIGH = lax.Precision.HIGHEST
BETA = 0.5
RATE = 0.5
EPS = 1e-12
MASKED = -1e30


def gelu_exact(values):
    return jax.nn.gelu(values, approximate=False)


def normalize(summed, gain_in, offset, hidden_gate):
    centre = summed - jnp.mean(summed, axis=-1, keepdims=True)
    spread = jnp.mean(centre * centre, axis=-1, keepdims=True)
    return (centre * lax.rsqrt(spread + EPS) * gain_in + offset) * hidden_gate


def split_heads(block_joined, head_count):
    pieces = block_joined.reshape(block_joined.shape[0], 3, head_count, -1)
    return (pieces[:, 0], pieces[:, 1], pieces[:, 2])


def masked_scores(queries, keys_in, labels, factor):
    scores = (
        jnp.einsum("qhd,khd->hqk", queries, keys_in, preferred_element_type=jnp.float32) * factor
    )
    allowed = labels[:, None] == labels[None, :]
    return jnp.where(allowed[None], scores, MASKED)


def attend_forward(packed, head_count, factor):
    block_joined, labels = packed
    queries, keys_in, values_in = split_heads(block_joined, head_count)
    scores = masked_scores(queries, keys_in, labels, factor)
    highest = jnp.max(scores, axis=-1, keepdims=True)
    raised = jnp.exp(scores - highest)
    totals = jnp.sum(raised, axis=-1, keepdims=True)
    weights_low = (raised / totals).astype(jnp.bfloat16)
    context = jnp.einsum("hqk,khd->qhd", weights_low, values_in, preferred_element_type=jnp.float32)
    return (context, (highest + jnp.log(totals))[:, :, 0])


def attend_backward(packed, head_count, factor):
    block_joined, log_totals, context_grad, labels = packed
    queries, keys_in, values_in = split_heads(block_joined, head_count)
    scores = masked_scores(queries, keys_in, labels, factor)
    weights_full = jnp.exp(scores - log_totals[:, :, None])
    weights_low = weights_full.astype(jnp.bfloat16)
    values_grad = jnp.einsum(
        "hqk,qhd->khd", weights_low, context_grad, preferred_element_type=jnp.float32
    )
    weights_grad = jnp.einsum(
        "qhd,khd->hqk", context_grad, values_in, preferred_element_type=jnp.float32
    )
    inner_sum = jnp.sum(weights_full * weights_grad, axis=-1, keepdims=True)
    scores_grad = (weights_full * (weights_grad - inner_sum)).astype(jnp.bfloat16)
    queries_grad = (
        jnp.einsum("hqk,khd->qhd", scores_grad, keys_in, preferred_element_type=jnp.float32)
        * factor
    )
    keys_grad = (
        jnp.einsum("hqk,qhd->khd", scores_grad, queries, preferred_element_type=jnp.float32)
        * factor
    )
    merged = jnp.concatenate([queries_grad, keys_grad, values_grad], axis=1)
    return merged.reshape(merged.shape[0], -1).astype(jnp.bfloat16)


def contract_rows(left, right):
    return lax.dot_general(
        left, right, (((0,), (0,)), ((), ())), preferred_element_type=jnp.float32
    )


def contract_cols(left, right):
    return lax.dot_general(
        left, right, (((1,), (1,)), ((), ())), preferred_element_type=jnp.float32
    )


def body(
    tokens,
    segments,
    head_mask,
    unit_mask,
    hidden_mask,
    layer_gates,
    qkv_weight,
    out_weight,
    norm_gain,
    norm_bias,
    up_weight,
    down_weight,
    cotangent,
    owner_slot,
    master,
    left_stats,
    right_stats,
    left_root,
    right_root,
):
    row_count = tokens.shape[0]
    width = tokens.shape[1]
    head_count = head_mask.shape[0]
    head_width = width // head_count
    block_rows = segments.shape[1]
    block_count = segments.shape[0]
    factor = 1.0 / math.sqrt(head_width)
    model_size = lax.axis_size("mp")
    share = FF // model_size
    part_rows = SB // model_size
    total_tokens = row_count * lax.axis_size("dp") * model_size
    head_gate = head_mask.astype(jnp.float32)
    unit_gate = unit_mask.astype(jnp.float32)
    hidden_gate = hidden_mask.astype(jnp.float32)
    inputs = tokens.astype(jnp.float32)
    back_full = cotangent.astype(jnp.float32)
    qkv_full, out_full, up_full, down_full = (
        lax.all_gather(qkv_weight, "mp", axis=0, tiled=True),
        lax.all_gather(out_weight, "mp", axis=0, tiled=True),
        lax.all_gather(up_weight, "mp", axis=1, tiled=True),
        lax.all_gather(down_weight, "mp", axis=1, tiled=True),
    )
    joined_qkv = jnp.dot(tokens, qkv_full, preferred_element_type=jnp.float32).astype(jnp.bfloat16)
    joined_blocks = joined_qkv.reshape(block_count, block_rows, 3 * width)
    context, log_totals = lax.map(
        partial(attend_forward, head_count=head_count, factor=factor), (joined_blocks, segments)
    )
    context = context.reshape(row_count, head_count, head_width)
    gated_low = (context * head_gate[None, :, None]).reshape(row_count, width).astype(jnp.bfloat16)
    attn_out = jnp.dot(gated_low, out_full, preferred_element_type=jnp.float32)
    summed = inputs + layer_gates[0] * attn_out
    hidden, norm_pull = jax.vjp(normalize, summed, norm_gain, norm_bias, hidden_gate)
    hidden_low = hidden.astype(jnp.bfloat16)
    pre_act = jnp.dot(hidden_low, up_full, preferred_element_type=jnp.float32)
    active, gelu_pull = jax.vjp(gelu_exact, pre_act)
    active_low = (active * unit_gate).astype(jnp.bfloat16)
    branch = contract_cols(active_low, down_full)
    output = (hidden + layer_gates[1] * branch).astype(jnp.bfloat16)
    back_rounded = (layer_gates[1] * back_full).astype(jnp.bfloat16)
    qkv_full, out_full, up_full, down_full = (
        lax.all_gather(qkv_weight, "mp", axis=0, tiled=True),
        lax.all_gather(out_weight, "mp", axis=0, tiled=True),
        lax.all_gather(up_weight, "mp", axis=1, tiled=True),
        lax.all_gather(down_weight, "mp", axis=1, tiled=True),
    )
    grad_active = jnp.dot(back_rounded, down_full, preferred_element_type=jnp.float32)
    unit_grad = jnp.sum(grad_active * active, axis=0)
    grad_inner = gelu_pull(grad_active * unit_gate)[0].astype(jnp.bfloat16)
    hidden_back = contract_cols(grad_inner, up_full)
    up_term = contract_rows(grad_inner, hidden_low)
    down_term = contract_rows(active_low, back_rounded)
    unit_local = (
        lax.psum_scatter(
            jnp.stack([up_term, down_term], axis=1).astype(jnp.bfloat16),
            "mp",
            scatter_dimension=0,
            tiled=True,
        )
        .astype(jnp.float32)
        .transpose(1, 2, 0)
    )
    summed_grad, gain_grad, bias_grad, mask_grad = norm_pull(back_full + hidden_back)
    layer_grad = jnp.stack([jnp.sum(summed_grad * attn_out), jnp.sum(back_full * branch)])
    out_back = (layer_gates[0] * summed_grad).astype(jnp.bfloat16)
    gated_grad = contract_cols(out_back, out_full).astype(jnp.bfloat16)
    gated_heads = gated_grad.reshape(row_count, head_count, head_width)
    head_grad = jnp.sum(context * gated_heads.astype(jnp.float32), axis=(0, 2))
    context_grad = gated_heads * head_mask.astype(jnp.bfloat16)[None, :, None]
    joined_grad = lax.map(
        partial(attend_backward, head_count=head_count, factor=factor),
        (
            joined_blocks,
            log_totals,
            context_grad.reshape(block_count, block_rows, head_count, head_width),
            segments,
        ),
    )
    joined_grad = joined_grad.reshape(row_count, 3 * width)
    input_grad = summed_grad + contract_cols(joined_grad, qkv_full)
    tiles = width // SB
    qkv_term = jnp.einsum(
        "tri,tcj->rcij",
        tokens.reshape(row_count, tiles, SB),
        joined_grad.reshape(row_count, 3 * tiles, SB),
        preferred_element_type=jnp.float32,
    )
    out_term = jnp.einsum(
        "tri,tcj->rcij",
        gated_low.reshape(row_count, tiles, SB),
        out_back.reshape(row_count, tiles, SB),
        preferred_element_type=jnp.float32,
    )
    attn_terms = jnp.concatenate(
        [
            qkv_term.reshape(-1, model_size, part_rows, SB),
            out_term.reshape(-1, model_size, part_rows, SB),
        ],
        axis=0,
    )
    attn_rows = (
        lax.psum_scatter(attn_terms.astype(jnp.bfloat16), "mp", scatter_dimension=1, tiled=True)
        .astype(jnp.float32)
        .reshape(-1, part_rows, SB)
    )
    unit_split = unit_local.reshape(2, tiles, model_size, part_rows, share)
    unit_rows = lax.all_to_all(
        unit_split.astype(jnp.bfloat16), "mp", split_axis=2, concat_axis=4, tiled=True
    ).astype(unit_split.dtype)
    unit_rows = (
        unit_rows.reshape(2, tiles, part_rows, FF // SB, SB)
        .transpose(0, 1, 3, 2, 4)
        .reshape(-1, part_rows, SB)
    )
    all_rows = jnp.concatenate([attn_rows, unit_rows], axis=0)
    slot_order = jnp.argsort(owner_slot)
    slotted = jnp.take(all_rows, slot_order, axis=0)
    owned = lax.psum_scatter(
        slotted.astype(jnp.bfloat16), "dp", scatter_dimension=0, tiled=True
    ).astype(jnp.float32)
    full_grad = lax.all_gather(owned.astype(jnp.bfloat16), "mp", axis=1, tiled=True).astype(
        owned.dtype
    )
    row_start = lax.axis_index("mp") * part_rows
    columns = lax.dynamic_slice_in_dim(full_grad, row_start, part_rows, 2)
    left_new = BETA * left_stats + (1.0 - BETA) * jnp.einsum(
        "srj,skj->srk", owned, full_grad, precision=HIGH
    )
    right_new = BETA * right_stats + (1.0 - BETA) * jnp.einsum(
        "sjr,sjk->srk", columns, full_grad, precision=HIGH
    )
    left_part = jnp.einsum("sri,sij->srj", left_root, full_grad, precision=HIGH)
    update = jnp.einsum("srj,sjk->srk", left_part, right_root, precision=HIGH)
    weight_new = master - RATE * update
    norm_grad = jnp.stack([gain_grad, bias_grad])
    norm_grad, mask_grad, head_grad, layer_grad, unit_grad = lax.psum(
        (norm_grad, mask_grad, head_grad, layer_grad, unit_grad), ("dp", "mp")
    )
    norm_new = jnp.stack([norm_gain, norm_bias]) - 0.2 / math.sqrt(total_tokens) * norm_grad
    return (
        output,
        input_grad,
        head_grad,
        unit_grad,
        mask_grad,
        layer_grad,
        norm_grad,
        norm_new,
        owned,
        left_new,
        right_new,
        weight_new,
        weight_new.astype(jnp.bfloat16),
    )


def solution(mesh):
    return jax.shard_map(
        body,
        mesh=mesh,
        in_specs=(
            P(("dp", "mp"), None),
            P(("dp", "mp"), None),
            P(),
            P(),
            P(),
            P(),
            P("mp", None),
            P("mp", None),
            P(),
            P(),
            P(None, "mp"),
            P(None, "mp"),
            P(("dp", "mp"), None),
            P(),
            P("dp", "mp", None),
            P("dp", "mp", None),
            P("dp", "mp", None),
            P("dp", "mp", None),
            P("dp", None, None),
        ),
        out_specs=(
            P(("dp", "mp"), None),
            P(("dp", "mp"), None),
            P(),
            P(),
            P(),
            P(),
            P(),
            P(),
            P("dp", "mp", None),
            P("dp", "mp", None),
            P("dp", "mp", None),
            P("dp", "mp", None),
            P("dp", "mp", None),
        ),
        check_vma=False,
    )
```

profile of v0, /device:TPU:9, one launch (start us, length us, event | category | flops | bytes accessed | tf_op | source)
XLA Modules:
  0.0 669.6 jit_solution(17716247387969877652)
XLA Ops:
  19.7 22.3 %all-gather.6.cloned.1.call-done = bf16[768,2304]{1,0:T(8,128)(2,1)} async-done(((bf16[192,2304]{1,0:T(8,128)(2,1)}), bf16[768,2304]{1,0:T(8,128)(2,1)}) %all-gather.6.cloned.1.call-update) | async-done | bytes 3538960 | tf_op jit(solution)/shard_map/all_gather | solution.py:131
  42.0 8.4 %convolution_convert_fusion = bf16[1024,2304]{1,0:T(8,128)(2,1)} fusion(bf16[1024,768]{1,0:T(8,128)(2,1)} %param.23, bf16[768,2304]{1,0:T(8,128)(2,1)} %all-gather.6.cloned.1.call-done), kind=kOutput, calls=%fused_computation.70 | convolution fusion | flops 3626237952 | bytes 9830400 | tf_op jit(solution)/shard_map/dot_general | solution.py:136
  50.4 6.7 %copy.84 = bf16[2,512,2304]{1,2,0:T(8,128)(2,1)} copy(bf16[2,512,2304]{2,1,0:T(8,128)(2,1)} %bitcast.203) | data formatting | bytes 9437184 | tf_op jit(solution)/shard_map/while | solution.py:138
  57.1 28.8 %while.22 = (s32[]{:T(128)}, f32[2,512,12,64]{1,3,2,0:T(8,128)}, f32[2,12,512]{2,1,0:T(8,128)}, bf16[2,512,2304]{1,2,0:T(8,128)(2,1)}, s32[2,512]{1,0:T(2,128)S(1)}, /*index=5*/s32[]{:T(128)}) while((s32[]{:T(128)}, f32[2,512,12,64]{1,3,2,0:T(8,128)}, f32[2,12,512]{2,1,0:T(8,128)}, bf16[2,512,2304]{1,2,0:T(8,128)(2,1)}, ...), condition=%wide.region_3.4_spmd, body=%wide.region_0.3_spmd.sunk | while | flops 843311104 | bytes 58145924 | solution.py:138
  65.6 5.6 bitcast_dynamic-update-slice_fusion.4
  80.2 5.6 bitcast_dynamic-update-slice_fusion.4
  99.7 6.7 %fusion.57 = (f32[1024]{0:T(1024)S(1)}, f32[1024,768]{0,1:T(8,128)S(1)}, f32[1024,768]{0,1:T(8,128)}) fusion(f32[]{:T(128)} %bitcast.19, bf16[1024,768]{0,1:T(8,128)(2,1)} %copy.83, bf16[768,768]{1,0:T(8,128)(2,1)} %all-gather.8.cloned.1.call-done, f32[1024,768]{0,1:T(8,128)} %bitcast.196, f32[768]{0:T(1024)S(1)} %mul.224), kind=kOutput, calls=%fused_computation.130 | convolution fusion | flops 1212677120 | bytes 12196868 | tf_op jit(solution)/shard_map/dot_general | solution.py:143
  109.1 12.2 %fusion.54 = f32[1024,3072]{1,0:T(8,128)} fusion(bf16[768,3072]{1,0:T(8,128)(2,1)} %all-gather.10.cloned.1.call-done, f32[1024,768]{0,1:T(8,128)} %copy-done.5, f32[768]{0:T(1024)S(1)} %copy-done.30, f32[768]{0:T(1024)} %param.32, f32[768]{0:T(1024)S(1)} %copy-done.27, f32[1024]{0:T(1024)S(1)} %fusion.52, f32[1024]{0:T(1024)S(1)} %broadcast_multiply_fusion.1), kind=kOutput, calls=%fused_computation.128 | convolution fusion | flops 4836556800 | bytes 20464640 | tf_op jit(solution)/shard_map/dot_general | solution.py:147
  121.3 17.7 %all-gather.12.cloned.1.call-done = bf16[768,3072]{1,0:T(8,128)(2,1)} async-done(((bf16[768,768]{1,0:T(8,128)(2,1)}), bf16[768,3072]{1,0:T(8,128)(2,1)}) %all-gather.12.cloned.1.call-update) | async-done | bytes 4718608 | tf_op jit(solution)/shard_map/all_gather | solution.py:134
  139.0 39.0 %multiply_reduce_fusion.1 = (f32[3072]{0:T(1024)}, f32[1024,3072]{1,0:T(8,128)}, f32[1024,3072]{1,0:T(8,128)}) fusion(f32[1024,3072]{1,0:T(8,128)} %fusion.54, bf16[768,3072]{1,0:T(8,128)(2,1)} %all-gather.12.cloned.1.call-done, bf16[1024,768]{0,1:T(8,128)(2,1)} %copy.87, f32[]{:T(128)} %bitcast.21), kind=kOutput, calls=%fused_computation.51 | convolution fusion | flops 5041812480 | bytes 44052484 | tf_op jit(solution)/shard_map/dot_general | solution.py:159
  178.1 16.6 %add_convert_fusion = (bf16[1024,3072]{1,0:T(8,128)(2,1)}, bf16[1024,3072]{1,0:T(8,128)(2,1)}) fusion(f32[1024,3072]{1,0:T(8,128)} %get-tuple-element.182, f32[1024,3072]{1,0:T(8,128)} %get-tuple-element.202, f32[1024,3072]{1,0:T(8,128)S(1)} %bitcast.193, f32[3072]{0:T(1024)S(1)} %copy-done.40), kind=kLoop, calls=%fused_computation.52 | loop fusion | flops 56623104 | bytes 50343936 | tf_op jit(solution)/shard_map/convert_element_type | solution.py:161
  194.7 10.6 %fusion.36 = bf16[3072,1,768]{2,0,1:T(8,128)(2,1)} fusion(bf16[1024,3072]{1,0:T(8,128)(2,1)} %get-tuple-element.191, f32[1024,768]{0,1:T(8,128)S(1)} %copy-done.6, f32[768]{0:T(1024)S(1)} %copy-done.31, f32[768]{0:T(1024)S(1)} %copy-done.35, f32[768]{0:T(1024)S(1)} %copy-done.28, f32[1024]{0:T(1024)S(1)} %copy-done.33, f32[1024]{0:T(1024)S(1)} %copy-done.26), kind=kOutput, calls=%fused_computation.80 | convolution fusion | flops 4838916096 | bytes 14173184 | tf_op jit(solution)/shard_map/dot_general | solution.py:82
  205.3 7.9 %fusion.37 = bf16[3072,1,768]{2,0,1:T(8,128)(2,1)} fusion(bf16[1024,3072]{1,0:T(8,128)(2,1)S(1)} %copy-done.13, bf16[1024,768]{0,1:T(8,128)(2,1)S(1)} %copy-done.17, f32[]{:T(128)} %bitcast.21), kind=kOutput, calls=%fused_computation.81 | convolution fusion | flops 4836556800 | bytes 12582916 | tf_op jit(solution)/shard_map/dot_general | solution.py:82
  213.3 8.2 %pad_maximum_fusion.1 = bf16[3072,2,768]{2,0,1:T(8,128)(2,1)} fusion(bf16[3072,1,768]{2,0,1:T(8,128)(2,1)} %fusion.37, bf16[3072,1,768]{2,0,1:T(8,128)(2,1)} %fusion.36), kind=kLoop, calls=%fused_computation.68 | loop fusion | flops 4718592 | bytes 18874368 | tf_op jit(solution)/shard_map/stack | solution.py:167
  221.6 8.7 %fusion.61 = f32[1024,768]{0,1:T(8,128)S(1)} fusion(bf16[1024,3072]{1,0:T(8,128)(2,1)} %get-tuple-element.192, bf16[768,3072]{1,0:T(8,128)(2,1)} %all-gather.12.cloned.1.call-done), kind=kOutput, calls=%fused_computation.134 | convolution fusion | flops 4831838208 | bytes 14155776 | tf_op jit(solution)/shard_map/dot_general | solution.py:88
  230.4 14.7 %multiply_reduce_fusion.2 = (f32[768]{0:T(1024)}, f32[1024]{0:T(1024)S(1)}, f32[768]{0:T(1024)}, f32[768]{0:T(1024)}, bf16[1024,768]{0,1:T(8,128)(2,1)}, /*index=5*/f32[]{:T(128)}, f32[1024,768]{0,1:T(8,128)S(1)}) fusion(f32[1024,768]{0,1:T(8,128)S(1)} %copy-done.7, f32[768]{0:T(1024)S(1)} %copy-done.31, f32[1024]{0:T(1024)S(1)} %copy-done.33, ...), kind=kOutput, calls=%fused_computation.87 | convolution fusion | flops 4848349184 | bytes 23623688 | tf_op jit(solution)/shard_map/dot_general | solution.py:88
  265.5 55.5 %while.23 = (s32[]{:T(128)}, bf16[2,512,2304]{1,2,0:T(8,128)(2,1)}, bf16[2,512,2304]{1,2,0:T(8,128)(2,1)}, s32[2,512]{1,0:T(2,128)S(1)}, f32[2,12,512]{2,1,0:T(8...) while((s32[]{:T(128)}, bf16[2,512,2304]{1,2,0:T(8,128)(2,1)}, bf16[2,512,2304]{1,2,0:T(8,128)(2,1)}, ...), condition=%wide.region_10.11_spmd, body=%wide.region_8.10_spmd.sunk | while | flops 2065033216 | bytes 142990544 | solution.py:182
  269.9 7.0 %multiply_reduce_fusion.10 = (f32[12,512]{1,0:T(8,128)S(1)}, f32[12,512,512]{1,2,0:T(8,128)}) fusion(f32[12,512,512]{1,2,0:T(8,128)S(1)} %fusion.106, f32[12,512]{1,0:T(8,128)S(1)} %dynamic-slice_bitcast_fusion.3, pred[512,512]{0,1:T(8,128)(4,1)S(1)} %broadcast_compare_fusion.5, bf16[512,3,12,64]{0,3,2,1:T(8,128)(2,1)S(1)} %bitcast.186, ...), kind=kOutput, calls=%fused_computation.19.clone.1 | convolution fusion | flops 418375680 | bytes 27058180 | tf_op jit(solution)/shard_map/while/body/eval_jaxpr/qhd,khd->hqk/dot_general | solution.py:64
  276.9 7.1 %multiply_convert_fusion.12 = bf16[12,512,512]{1,2,0:T(8,128)(2,1)S(1)} fusion(f32[12,512,512]{1,2,0:T(8,128)} %get-tuple-element.280, f32[12,512,512]{1,2,0:T(8,128)S(1)} %fusion.106, f32[12,512]{1,0:T(8,128)S(1)} %get-tuple-element.281, f32[12,512]{1,0:T(8,128)S(1)} %dynamic-slice_bitcast_fusion.3, pred[512,512]{0,1:T(8,128)(4,1)S(1)} %broadcast_compare_fusion.5), kind=kLoop, calls=%fused_computation.18.clone.1 | loop fusion | flops 18874368 | bytes 31768576 | tf_op jit(solution)/shard_map/while/body/eval_jaxpr/convert_element_type | solution.py:68
  297.5 7.0 %multiply_reduce_fusion.10 = (f32[12,512]{1,0:T(8,128)S(1)}, f32[12,512,512]{1,2,0:T(8,128)}) fusion(f32[12,512,512]{1,2,0:T(8,128)S(1)} %fusion.106, f32[12,512]{1,0:T(8,128)S(1)} %dynamic-slice_bitcast_fusion.3, pred[512,512]{0,1:T(8,128)(4,1)S(1)} %broadcast_compare_fusion.5, bf16[512,3,12,64]{0,3,2,1:T(8,128)(2,1)S(1)} %bitcast.186, ...), kind=kOutput, calls=%fused_computation.19.clone.1 | convolution fusion | flops 418375680 | bytes 27058180 | tf_op jit(solution)/shard_map/while/body/eval_jaxpr/qhd,khd->hqk/dot_general | solution.py:64
  304.5 7.1 %multiply_convert_fusion.12 = bf16[12,512,512]{1,2,0:T(8,128)(2,1)S(1)} fusion(f32[12,512,512]{1,2,0:T(8,128)} %get-tuple-element.280, f32[12,512,512]{1,2,0:T(8,128)S(1)} %fusion.106, f32[12,512]{1,0:T(8,128)S(1)} %get-tuple-element.281, f32[12,512]{1,0:T(8,128)S(1)} %dynamic-slice_bitcast_fusion.3, pred[512,512]{0,1:T(8,128)(4,1)S(1)} %broadcast_compare_fusion.5), kind=kLoop, calls=%fused_computation.18.clone.1 | loop fusion | flops 18874368 | bytes 31768576 | tf_op jit(solution)/shard_map/while/body/eval_jaxpr/convert_element_type | solution.py:68
  321.0 9.9 %copy.95 = bf16[2,512,2304]{1,0,2:T(2,128)(2,1)} copy(bf16[2,512,2304]{1,2,0:T(8,128)(2,1)} %get-tuple-element.76) | data formatting | bytes 9437184 | tf_op jit(solution)/shard_map/while | solution.py:182
  330.9 8.7 %reshape_reshape.3 = bf16[1024,6,384]{0,2,1:T(8,128)(2,1)} reshape(bf16[2,512,2304]{1,0,2:T(2,128)(2,1)} %copy.95) | data formatting | bytes 9437184 | tf_op jit(solution)/shard_map/reshape;reshape | solution.py:197
  339.6 6.8 %convert_bitcast_fusion = bf16[2,6,384,384]{3,2,0,1:T(8,128)(2,1)S(1)} fusion(bf16[1024,2,384,1]{0,2,1,3:T(8,128)(2,1)} %bitcast.200, bf16[1024,6,384]{0,2,1:T(8,128)(2,1)} %reshape_reshape.3), kind=kOutput, calls=%fused_computation.83 | convolution fusion | flops 3625648128 | bytes 9830400 | tf_op jit(solution)/shard_map/tri,tcj->rcij/dot_general | solution.py:194
  367.7 103.8 %all-reduce.4.cloned.1.call-done = bf16[16,4,96,384]{3,2,1,0:T(8,128)(2,1)} async-done(((bf16[16,4,96,384]{3,2,1,0:T(8,128)(2,1)}), bf16[16,4,96,384]{3,2,1,0:T(8,128)(2,1)}) %all-reduce.4.cloned.1.call-update) | async-done | bytes 4718608
  479.4 5.2 convert_element_type.132
  488.8 5.1 gather_fusion
  499.0 79.6 %reduce-scatter.8.cloned.1.call-done = bf16[6,96,384]{2,1,0:T(8,128)(2,1)} async-done(((bf16[48,96,384]{2,1,0:T(8,128)(2,1)}), bf16[6,96,384]{2,1,0:T(8,128)(2,1)}) %reduce-scatter.8.cloned.1.call-update) | async-done | bytes 442384 | tf_op jit(solution)/shard_map/reduce_scatter | solution.py:230
  581.9 5.5 multiply_reduce_fusion.5
  587.4 39.9 %all-reduce.1 = (f32[12]{0:T(128)}, f32[3072]{0:T(1024)}, f32[768]{0:T(1024)}, f32[2]{0:T(128)}, f32[2,768]{1,0:T(2,128)}) all-reduce(f32[12]{0:T(128)} %multiply_reduce_fusion.5, f32[3072]{0:T(1024)} %get-tuple-element.181, f32[768]{0:T(1024)} %get-tuple-element.152, ...), channel_id=1, replica_groups=mesh['dp'=8,'mp'=4] {'dp','mp'}, use_global_device_ids=true, to_apply=%region_12.13 | all-reduce | flops 5390 | bytes 43120 | tf_op jit(solution)/shard_map/psum | solution.py:248
  627.2 6.7 copy.91
  633.9 9.8 %add_add_fusion.1 = f32[1024,768]{0,1:T(8,128)} fusion(f32[1024,768]{0,1:T(8,128)} %copy-done.11, bf16[1024,2304]{1,0:T(8,128)(2,1)} %bitcast.202, bf16[768,2304]{1,0:T(8,128)(2,1)} %all-gather.6.cloned.1.call-done, f32[1024]{0:T(1024)S(1)} %copy-done.44), kind=kOutput, calls=%fused_computation.99 | convolution fusion | flops 3625451520 | bytes 14553088 | tf_op jit(solution)/shard_map/dot_general | solution.py:88
  (238 shorter events, 153.7 us)
Async XLA Ops:
  7.2 648.2 %copy-start = (f32[6,384,384]{2,1,0:T(8,128)S(1)}, f32[6,384,384]{2,1,0:T(8,128)}, u32[]{:S(2)}) copy-start(f32[6,384,384]{2,1,0:T(8,128)} %param.41) | copy-start | bytes 10616836
  7.2 34.8 %all-gather.6.cloned.1.call-start = ((), (), s32[]{:S(2)}) async-start(), calls=%async_computation.3 | async-start | bytes 4423680 | tf_op jit(solution)/shard_map/all_gather | solution.py:131
  7.9 91.8 %all-gather.8.cloned.1.call-start = ((), (), s32[]{:S(2)}) async-start(), calls=%async_computation.4 | async-start | bytes 1474560 | tf_op jit(solution)/shard_map/all_gather | solution.py:132
  8.7 100.4 %all-gather.10.cloned.1.call-start = ((), (), s32[]{:S(2)}) async-start(), calls=%async_computation.5 | async-start | bytes 5898240 | tf_op jit(solution)/shard_map/all_gather | solution.py:133
  9.4 129.6 %all-gather.12.cloned.1.call-start = ((), (), s32[]{:S(2)}) async-start(), calls=%async_computation.6 | async-start | bytes 5898240 | tf_op jit(solution)/shard_map/all_gather | solution.py:134
  10.0 342.6 %reduce-scatter.6.cloned.1.call-start = ((), (), s32[]{:S(2)}) async-start(), calls=%async_computation.7 | async-start | bytes 11796480 | tf_op jit(solution)/shard_map/reduce_scatter | solution.py:166
  99.7 9.4 %copy-start.27 = (f32[768]{0:T(1024)S(1)}, f32[768]{0:T(1024)}, u32[]{:S(2)}) copy-start(f32[768]{0:T(1024)} %param.31) | copy-start | bytes 9220
  99.7 9.4 %copy-start.30 = (f32[768]{0:T(1024)S(1)}, f32[768]{0:T(1024)}, u32[]{:S(2)}) copy-start(f32[768]{0:T(1024)} %convert_element_type.114) | copy-start | bytes 9220
  106.5 14.8 %copy-start.25 = (f32[1024]{0:T(1024)}, f32[1024]{0:T(1024)S(1)}, u32[]{:S(2)}) copy-start(f32[1024]{0:T(1024)S(1)} %broadcast_multiply_fusion.1) | copy-start | bytes 12292
  109.1 12.3 %copy-start.32 = (f32[1024]{0:T(1024)}, f32[1024]{0:T(1024)S(1)}, u32[]{:S(2)}) copy-start(f32[1024]{0:T(1024)S(1)} %fusion.52) | copy-start | bytes 12292
  139.0 39.0 %slice-start = ((s8[12582912]{0:T(1024)(128)(4,1)}), s8[4194304]{0:T(1024)(128)(4,1)S(1)}, s32[]{:S(2)}) async-start(s8[12582912]{0:T(1024)(128)(4,1)} %bitcast.192), calls=%async_computation.11 | async-start | bytes 8388608
  139.0 39.0 %slice-start.1 = ((s8[12582912]{0:T(1024)(128)(4,1)}), s8[4194304]{0:T(1024)(128)(4,1)S(1)}, s32[]{:S(2)}) async-start(s8[12582912]{0:T(1024)(128)(4,1)} %bitcast.192), calls=%async_computation.12 | async-start | bytes 8388608
  139.0 39.0 %slice-start.2 = ((s8[12582912]{0:T(1024)(128)(4,1)}), s8[4194304]{0:T(1024)(128)(4,1)S(1)}, s32[]{:S(2)}) async-start(s8[12582912]{0:T(1024)(128)(4,1)} %bitcast.192), calls=%async_computation.13 | async-start | bytes 8388608
  139.0 39.0 %copy-start.40 = (f32[3072]{0:T(1024)S(1)}, f32[3072]{0:T(1024)}, u32[]{:S(2)}) copy-start(f32[3072]{0:T(1024)} %convert_element_type.116) | copy-start | bytes 36868
  178.0 16.7 %copy-start.6 = (f32[1024,768]{0,1:T(8,128)S(1)}, f32[1024,768]{0,1:T(8,128)}, u32[]{:S(2)}) copy-start(f32[1024,768]{0,1:T(8,128)} %copy-done.5) | copy-start | bytes 9437188
  178.0 16.7 %copy-start.26 = (f32[1024]{0:T(1024)S(1)}, f32[1024]{0:T(1024)}, u32[]{:S(2)}) copy-start(f32[1024]{0:T(1024)} %copy-done.25) | copy-start | bytes 12292
  178.0 16.6 %copy-start.28 = (f32[768]{0:T(1024)S(1)}, f32[768]{0:T(1024)}, u32[]{:S(2)}) copy-start(f32[768]{0:T(1024)} %param.31) | copy-start | bytes 9220
  178.0 16.6 %copy-start.31 = (f32[768]{0:T(1024)S(1)}, f32[768]{0:T(1024)}, u32[]{:S(2)}) copy-start(f32[768]{0:T(1024)} %convert_element_type.114) | copy-start | bytes 9220
  178.0 16.6 %copy-start.33 = (f32[1024]{0:T(1024)S(1)}, f32[1024]{0:T(1024)}, u32[]{:S(2)}) copy-start(f32[1024]{0:T(1024)} %copy-done.32) | copy-start | bytes 12292
  178.1 16.6 %copy-start.35 = (f32[768]{0:T(1024)S(1)}, f32[768]{0:T(1024)}, u32[]{:S(2)}) copy-start(f32[768]{0:T(1024)} %param.32) | copy-start | bytes 9220
  194.7 10.6 %copy-start.13 = (bf16[1024,3072]{1,0:T(8,128)(2,1)S(1)}, bf16[1024,3072]{1,0:T(8,128)(2,1)}, u32[]{:S(2)}) copy-start(bf16[1024,3072]{1,0:T(8,128)(2,1)} %get-tuple-element.192) | copy-start | bytes 18874372
  194.7 10.6 %copy-start.17 = (bf16[1024,768]{0,1:T(8,128)(2,1)S(1)}, bf16[1024,768]{0,1:T(8,128)(2,1)}, u32[]{:S(2)}) copy-start(bf16[1024,768]{0,1:T(8,128)(2,1)} %copy.87) | copy-start | bytes 4718596
  221.5 250.0 %all-reduce.4.cloned.1.call-start = ((), (), s32[]{:S(2)}) async-start(), calls=%async_computation.10 | async-start | bytes 9437184
  221.5 8.8 %copy-start.7 = (f32[1024,768]{0,1:T(8,128)S(1)}, f32[1024,768]{0,1:T(8,128)}, u32[]{:S(2)}) copy-start(f32[1024,768]{0,1:T(8,128)} %copy-done.5) | copy-start | bytes 9437188
  221.6 8.8 %copy-start.18 = (bf16[1024,768]{0,1:T(8,128)(2,1)S(1)}, bf16[1024,768]{0,1:T(8,128)(2,1)}, u32[]{:S(2)}) copy-start(bf16[1024,768]{0,1:T(8,128)(2,1)} %copy.87) | copy-start | bytes 4718596
  221.6 8.8 %copy-start.36 = (f32[768]{0:T(1024)S(1)}, f32[768]{0:T(1024)}, u32[]{:S(2)}) copy-start(f32[768]{0:T(1024)} %param.32) | copy-start | bytes 9220
  230.3 14.8 %copy-start.42 = (f32[1024]{0:T(1024)S(1)}, f32[1024]{0:T(1024)}, u32[]{:S(2)}) copy-start(f32[1024]{0:T(1024)} %copy-done.41) | copy-start | bytes 12292
  360.4 114.1 %all-to-all-start = ((bf16[2,2,4,96,768]{4,3,1,0,2:T(8,128)(2,1)}), bf16[2,2,4,96,768]{4,3,1,0,2:T(8,128)(2,1)}, u32[]{:S(2)}, u32[]{:S(2)}) async-start(bf16[2,2,4,96,768]{4,3,1,0,2:T(8,128)(2,1)} %copy.103), calls=%async_computation.1 | async-start | bytes 4718592 | tf_op jit(solution)/shard_map/all_to_all | solution.py:219
  365.0 213.5 %reduce-scatter.8.cloned.1.call-start = ((), (), s32[]{:S(2)}) async-start(), calls=%async_computation.8 | async-start | bytes 3981312 | tf_op jit(solution)/shard_map/reduce_scatter | solution.py:230
  498.9 79.7 %copy-start.29 = (f32[768]{0:T(1024)S(1)}, f32[768]{0:T(1024)}, u32[]{:S(2)}) copy-start(f32[768]{0:T(1024)} %param.31) | copy-start | bytes 9220
  498.9 79.7 %copy-start.37 = (f32[768]{0:T(1024)S(1)}, f32[768]{0:T(1024)}, u32[]{:S(2)}) copy-start(f32[768]{0:T(1024)} %param.32) | copy-start | bytes 9220
  498.9 153.6 %all-gather.14.cloned.1.call-start = ((), (), s32[]{:S(2)}) async-start(), calls=%async_computation.9 | async-start | bytes 2211840 | tf_op jit(solution)/shard_map/all_gather | solution.py:233
  (39 other events, 137.0 us)
Sparse Core Ops, SparseCore 0:
  9.6 32.3 all-gather.5
  43.5 17.4 all-gather.7
  62.6 37.4 all-gather.9
  101.5 37.4 all-gather.11
  221.6 78.0 reduce-scatter.5
  352.7 118.6 all-reduce.3
  499.0 79.4 reduce-scatter.7
  580.1 21.2 all-gather.13
where the time goes:
time: 683 us; the launch traced here: 670 us
  waiting for transfers between devices  226 us (33%)
  matrix products  187 us (27%)
  local copies, waits for them, and re-layouts  116 us (17%)
  other arithmetic  80.2 us (12%)
  blocking collectives  39.9 us (6%)
  between operations  15.2 us (2%)
    unnamed x9, waiting for transfers between devices  106 us
    reduce_scatter x1, waiting for transfers between devices, body(): lax.psum_scatter(slotted.astype(jnp.bfloat16), 'dp', scatter_dimension=0,...  79.6 us
    psum x1, blocking collectives, body(): lax.psum((norm_grad, mask_grad, head_grad, layer_grad, unit_grad), ('dp',...  39.9 us
    dot_general x1, matrix products, body(): jnp.dot(back_rounded, down_full, preferred_element_type=jnp.float32)  39 us
    dot_general x4, matrix products, contract_cols(): lax.dot_general(left, right, (((1,), (1,)), ((), ())), preferred_element_...  35.9 us
    all_gather x1, waiting for transfers between devices, body(): lax.all_gather(qkv_weight, 'mp', axis=0, tiled=True)  22.3 us
    unnamed x106, local copies, waits for them, and re-layouts  22.1 us
    dot_general x2, matrix products, contract_rows(): lax.dot_general(left, right, (((0,), (0,)), ((), ())), preferred_element_...  18.5 us
  transfers between devices with their start and end apart: 9, of which 4 were waited for; matrix products, arithmetic and copies ran while one was open for 39% of the time, Pallas kernels for 0%

commit v1 on v0

--- a/solution.py
+++ b/solution.py
@@ -4,6 +4,8 @@
 import jax
 import jax.numpy as jnp
 from jax import lax
+from jax.experimental import pallas as pl
+from jax.experimental.pallas import tpu as pltpu
 from jax.sharding import PartitionSpec as P
 
 FF = 3072
@@ -225,8 +227,10 @@
         .reshape(-1, part_rows, SB)
     )
     all_rows = jnp.concatenate([attn_rows, unit_rows], axis=0)
-    slot_order = jnp.argsort(owner_slot)
-    slotted = jnp.take(all_rows, slot_order, axis=0)
+    slot_count = owner_slot.shape[0]
+    pick = (owner_slot[None, :] == jnp.arange(slot_count)[:, None]).astype(jnp.bfloat16)
+    flat_rows = all_rows.astype(jnp.bfloat16).reshape(slot_count, -1)
+    slotted = jnp.dot(pick, flat_rows, preferred_element_type=jnp.float32).reshape(all_rows.shape)
     owned = lax.psum_scatter(
         slotted.astype(jnp.bfloat16), "dp", scatter_dimension=0, tiled=True
     ).astype(jnp.float32)
@@ -266,9 +270,587 @@
     )
 
 
+F32 = jnp.float32
+BF = jnp.bfloat16
+MESH = pl.DeviceIdType.MESH
+LOG2E = 1.4426950408889634
+ROWS = 1024
+D = 768
+HD = 64
+BLK = 512
+NT_DIMS = (((1,), (1,)), ((), ()))
+NN_DIMS = (((1,), (0,)), ((), ()))
+
+
+def nn(left, right):
+    return lax.dot_general(left, right, NN_DIMS, preferred_element_type=F32)
+
+
+def nt(left, right):
+    return lax.dot_general(left, right, NT_DIMS, preferred_element_type=F32)
+
+
+def coords():
+    d = lax.axis_index("dp")
+    m = lax.axis_index("mp")
+    return d // 2, d % 2, m // 2, m % 2
+
+
+def at(z, x, y, c):
+    return (2 * z + x, 2 * y + c)
+
+
+def gelu_parts(x):
+    ax = jnp.abs(x)
+    e = jnp.exp2(x * x * (-0.5 * LOG2E))
+    t = 1.0 / (1.0 + (0.3275911 * math.sqrt(0.5)) * ax)
+    poly = t * (
+        0.5 * 0.254829592
+        + t
+        * (
+            -0.5 * 0.284496736
+            + t * (0.5 * 1.421413741 + t * (-0.5 * 1.453152027 + t * (0.5 * 1.061405429)))
+        )
+    )
+    tail = poly * e
+    cdf = jnp.where(x < 0, tail, 1.0 - tail)
+    active = x * cdf
+    return active, cdf + x * (e * (1.0 / math.sqrt(2.0 * math.pi)))
+
+
+def colsum(v):
+    return jnp.sum(v, axis=0, keepdims=True)
+
+
+def row_norm(summed):
+    centre = summed - jnp.mean(summed, axis=-1, keepdims=True)
+    spread = jnp.mean(centre * centre, axis=-1, keepdims=True)
+    inv = lax.rsqrt(spread + EPS)
+    return centre * inv, inv
+
+
+NPIECE = 6
+
+
+def forward_kernel(
+    gates,
+    tokens,
+    cot,
+    segcol,
+    segrow,
+    hgate,
+    ugate,
+    mgate,
+    gain,
+    bias,
+    qkv_in,
+    out_in,
+    up_in,
+    down_in,
+    o_out,
+    o_joined,
+    o_ctx,
+    o_ctxT,
+    o_tokT,
+    o_sgrad,
+    o_grad,
+    o_wq,
+    o_wo,
+    lse,
+    small,
+    wq,
+    wo,
+    wu,
+    wd,
+    joined,
+    ctx,
+    ctxT,
+    tokT,
+    attn,
+    hlow,
+    hT,
+    blow,
+    bT,
+    branch,
+    hback,
+    act,
+    inner,
+    grads,
+    outv,
+    send_sem,
+    recv_sem,
+    loc_sem,
+    out_sem,
+    grad_sem,
+):
+    z, x, y, c = coords()
+    m = 2 * y + c
+    ms = 2 * y + 1 - c
+    my = 2 * (1 - y) + c
+    mys = 2 * (1 - y) + 1 - c
+    sib = at(z, x, y, 1 - c)
+    ypeer = at(z, x, 1 - y, c)
+    xpeer = at(z, 1 - x, y, c)
+    g0 = gates[0]
+    g1 = gates[1]
+
+    barrier = pltpu.get_barrier_semaphore()
+    for peer in (sib, ypeer, xpeer):
+        pl.semaphore_signal(barrier, inc=1, device_id=peer, device_id_type=MESH)
+    pl.semaphore_wait(barrier, 3)
+
+    def full(j, i, h=None):
+        if j < 3:
+            ref, n, cols = wq, 192, pl.ds(768 * j, 768)
+        else:
+            ref, n, cols = ((wo, 192), (wu, 768), (wd, 768))[j - 3] + (slice(None),)
+        if h is None:
+            return ref.at[i, :, cols]
+        return ref.at[i, pl.ds(pl.multiple_of(h * (n // 2), 16), n // 2), cols]
+
+    def own(j, h=None):
+        if j < 3:
+            ref, n, cols = qkv_in, 192, pl.ds(768 * j, 768)
+        else:
+            ref, n, cols = ((out_in, 192), (up_in, 768), (down_in, 768))[j - 3] + (slice(None),)
+        if h is None:
+            return ref.at[:, cols]
+        return ref.at[pl.ds(pl.multiple_of(h * (n // 2), 16), n // 2), cols]
+
+    def remote(src, dst, j, k, dev):
+        return pltpu.make_async_remote_copy(
+            src_ref=src,
+            dst_ref=dst,
+            send_sem=send_sem.at[j, k],
+            recv_sem=recv_sem.at[j, k],
+            device_id=dev,
+            device_id_type=MESH,
+        )
+
+    def s1(j):
+        return remote(own(j), full(j, m), j, 0, sib)
+
+    def s2(j):
+        return remote(own(j, x), full(j, m, x), j, 1, ypeer)
+
+    def s3(j):
+        return remote(full(j, my, x), full(j, my, x), j, 2, xpeer)
+
+    def s4(j):
+        return remote(full(j, my, x), full(j, my, x), j, 3, sib)
+
+    def s5(j):
+        return remote(full(j, my, 1 - x), full(j, my, 1 - x), j, 4, sib)
+
+    def local(j):
+        return pltpu.make_async_copy(own(j), full(j, m), loc_sem.at[j])
+
+    def first(j):
+        s2(j).start()
+        s1(j).start()
+        local(j).start()
+
+    def second(j):
+        s2(j).wait_recv()
+        s3(j).start()
+        s4(j).start()
+
+    def third(j):
+        s3(j).wait_recv()
+        s5(j).start()
+
+    def finish_near(j):
+        local(j).wait()
+        s1(j).wait_recv()
+
+    def finish_far(j):
+        s4(j).wait_recv()
+        s5(j).wait_recv()
+
+    def finish_sends(j):
+        for s in (s1, s2, s3, s4, s5):
+            s(j).wait_send()
+
+    for j in range(3):
+        first(j)
+
+    tokT[...] = tokens[...].T
+    tok_copy = pltpu.make_async_copy(tokT, o_tokT, out_sem.at[0])
+    tok_copy.start()
+
+    @pl.loop(0, 4)
+    def _(r):
+        rows = pl.ds(pl.multiple_of(r * 256, 256), 256)
+        low = (g1 * cot[rows, :].astype(F32)).astype(BF)
+        blow[rows, :] = low
+        bT[:, rows] = low.T
+
+    second(0)
+    second(1)
+    third(0)
+    second(2)
+    third(1)
+    third(2)
+    for j in range(3, NPIECE):
+        first(j)
+    for j in range(3):
+        finish_near(j)
+        finish_far(j)
+    wq_copy = pltpu.make_async_copy(wq, o_wq, out_sem.at[1])
+    wq_copy.start()
+
+    for j in range(3):
+
+        @pl.loop(0, 4)
+        def _(r, j=j):
+            rows = pl.ds(pl.multiple_of(r * 256, 256), 256)
+            w = wq[:, :, pl.ds(768 * j, 768)].reshape(D, D)
+            joined[rows, pl.ds(768 * j, 768)] = nn(tokens[rows, :], w).astype(BF)
+
+    joined_copy = pltpu.make_async_copy(joined, o_joined, out_sem.at[2])
+    joined_copy.start()
+
+    scale = LOG2E / math.sqrt(HD)
+    half_iota = lax.broadcasted_iota(jnp.int32, (1, 128), 1) // HD
+    halves = [(half_iota == e).astype(F32).astype(BF) for e in range(2)]
+
+    def attend(i):
+        b = i // 6
+        p = i % 6
+        rows = pl.ds(pl.multiple_of(b * BLK, BLK), BLK)
+        lane = pl.multiple_of(p * 128, 128)
+        q = joined[rows, pl.ds(lane, 128)]
+        k = joined[rows, pl.ds(D + lane, 128)]
+        v = joined[rows, pl.ds(2 * D + lane, 128)]
+        sc = segcol[b]
+        sr = segrow[b]
+        for qt in range(2):
+            cols = slice(qt * 256, qt * 256 + 256)
+            allowed = sc == sr[:, cols]
+            total = None
+            for e in range(2):
+                s = nt(k * halves[e], q[cols, :])
+                s = jnp.where(allowed, s * scale, MASKED)
+                top = jnp.max(s, axis=0, keepdims=True)
+                pr = jnp.exp2(s - top)
+                tot = jnp.sum(pr, axis=0, keepdims=True)
+                low = (pr * (1.0 / tot)).astype(BF)
+                lse[2 * i + e, :, pl.ds(qt * 256, 256)] = top + jnp.log(tot) * LOG2E
+                part = nn((v * halves[e]).T, low)
+                total = part if total is None else total + part
+            qrows = pl.ds(pl.multiple_of(b * BLK + qt * 256, 256), 256)
+            ctxT[pl.ds(lane, 128), qrows] = total.astype(BF)
+            ctx[qrows, pl.ds(lane, 128)] = total.T.astype(BF)
+
+    pl.loop(0, 3)(attend)
+    second(3)
+    pl.loop(3, 5)(attend)
+    third(3)
+    pl.loop(5, 10)(attend)
+    second(4)
+    pl.loop(10, 12)(attend)
+    ctx_copy = pltpu.make_async_copy(ctx, o_ctx, out_sem.at[3])
+    ctx_copy.start()
+    ctxT_copy = pltpu.make_async_copy(ctxT, o_ctxT, out_sem.at[4])
+    ctxT_copy.start()
+    finish_near(3)
+    finish_far(3)
+    wo_copy = pltpu.make_async_copy(wo, o_wo, out_sem.at[5])
+    wo_copy.start()
+
+    @pl.loop(0, 4)
+    def _(r):
+        rows = pl.ds(pl.multiple_of(r * 256, 256), 256)
+        gated = ctx[rows, :] * hgate[...].astype(BF)
+        a = nn(gated, wo[...].reshape(D, D))
+        attn[rows, :] = a
+        normed, _ = row_norm(tokens[rows, :].astype(F32) + g0 * a)
+        low = ((normed * gain[...] + bias[...]) * mgate[...]).astype(BF)
+        hlow[rows, :] = low
+        hT[:, rows] = low.T
+
+    third(4)
+    second(5)
+
+    small[...] = jnp.zeros_like(small)
+
+    def feed(u, begin, slot):
+        if not begin:
+            pass
+        w_up = wu.at[u]
+        w_down = wd.at[u]
+
+        @pl.loop(0, 4)
+        def _(r):
+            rows = pl.ds(pl.multiple_of(r * 256, 256), 256)
+            pre = nn(hlow[rows, :], w_up[...])
+            back = nn(blow[rows, :], w_down[...])
+            active, slope = gelu_parts(pre)
+            gate = ugate[u]
+            small[pl.ds(u, 1), :] += colsum(back * active)
+            a_low = (active * gate).astype(BF)
+            i_low = (back * gate * slope).astype(BF)
+            act[rows, :] = a_low
+            inner[rows, :] = i_low
+            up_part = nt(a_low, w_down[...])
+            back_part = nt(i_low, w_up[...])
+            if begin:
+                branch[rows, :] = up_part
+                hback[rows, :] = back_part
+            else:
+                branch[rows, :] += up_part
+                hback[rows, :] += back_part
+
+        for which, (left, right) in enumerate(((hT, inner), (bT, act))):
+
+            @pl.loop(0, 8)
+            def _(t, which=which, left=left, right=right):
+                rr = pl.ds(pl.multiple_of(t * 96, 16), 96)
+                g = nn(left[rr, :], right[...]).astype(BF)
+                for j in range(2):
+                    for h in range(2):
+                        grads[slot, which, t // 4, j, t % 4 * 2 + h] = g[
+                            48 * h : 48 * h + 48, 384 * j : 384 * j + 384
+                        ]
+
+    def grad_copies(u, slot):
+        found = []
+        for which in range(2):
+            for r in range(2):
+                found.append(
+                    pltpu.make_async_copy(
+                        grads.at[slot, which, r],
+                        o_grad.at[which, r, pl.ds(2 * u, 2)],
+                        grad_sem.at[slot, which, r],
+                    )
+                )
+        return found
+
+    finish_near(4)
+    finish_near(5)
+    feed(m, True, 0)
+    for g in grad_copies(m, 0):
+        g.start()
+    third(5)
+    feed(ms, False, 1)
+    for g in grad_copies(ms, 1):
+        g.start()
+    finish_far(4)
+    finish_far(5)
+    for g in grad_copies(m, 0):
+        g.wait()
+    feed(my, False, 0)
+    for g in grad_copies(my, 0):
+        g.start()
+    for g in grad_copies(ms, 1):
+        g.wait()
+    feed(mys, False, 1)
+    for g in grad_copies(mys, 1):
+        g.start()
+
+    lane = lax.broadcasted_iota(jnp.int32, (1, D), 1)
+
+    @pl.loop(0, 4)
+    def _(r):
+        rows = pl.ds(pl.multiple_of(r * 256, 256), 256)
+        a = attn[rows, :]
+        normed, inv = row_norm(tokens[rows, :].astype(F32) + g0 * a)
+        plain = normed * gain[...] + bias[...]
+        back = cot[rows, :].astype(F32)
+        br = branch[rows, :]
+        outv[rows, :] = (plain * mgate[...] + g1 * br).astype(BF)
+        total = back + hback[rows, :]
+        masked = total * mgate[...]
+        small[4:5, :] += colsum(masked * normed)
+        small[5:6, :] += colsum(masked)
+        small[6:7, :] += colsum(total * plain)
+        n = masked * gain[...]
+        grad = (
+            n
+            - jnp.mean(n, axis=-1, keepdims=True)
+            - normed * jnp.mean(n * normed, axis=-1, keepdims=True)
+        ) * inv
+        hback[rows, :] = grad
+        small[7:8, :] += colsum(grad * a)
+        small[8:9, :] += colsum(back * br)
+
+    out_copy = pltpu.make_async_copy(outv, o_out, out_sem.at[6])
+    out_copy.start()
+    sgrad_copy = pltpu.make_async_copy(hback, o_sgrad, out_sem.at[7])
+    sgrad_copy.start()
+    for g in grad_copies(my, 0):
+        g.wait()
+    for g in grad_copies(mys, 1):
+        g.wait()
+    for copy in (tok_copy, wq_copy, joined_copy, ctx_copy, ctxT_copy, wo_copy, out_copy, sgrad_copy):
+        copy.wait()
+    for j in range(NPIECE):
+        finish_sends(j)
+
+
+def run_forward(gates, tokens, cot, segcol, segrow, hgate, ugate, mgate, gain, bias, qkv, out, up, down):
+    sds = jax.ShapeDtypeStruct
+    outs = (
+        sds((ROWS, D), BF),
+        sds((ROWS, 3 * D), BF),
+        sds((ROWS, D), BF),
+        sds((D, ROWS), BF),
+        sds((D, ROWS), BF),
+        sds((ROWS, D), F32),
+        sds((2, 2, 8, 8, 48, SB), BF),
+        sds((4, 192, 3 * D), BF),
+        sds((4, 192, D), BF),
+        sds((24, 1, BLK), F32),
+        sds((16, D), F32),
+    )
+    any_ = pl.BlockSpec(memory_space=pl.ANY)
+    vm = pl.BlockSpec(memory_space=pltpu.VMEM)
+    sm = pl.BlockSpec(memory_space=pltpu.SMEM)
+    return pl.pallas_call(
+        forward_kernel,
+        out_shape=outs,
+        in_specs=[sm] + [vm] * 9 + [any_] * 4,
+        out_specs=[any_] * 9 + [vm] * 2,
+        scratch_shapes=[
+            pltpu.VMEM((4, 192, 3 * D), BF),
+            pltpu.VMEM((4, 192, D), BF),
+            pltpu.VMEM((4, D, D), BF),
+            pltpu.VMEM((4, D, D), BF),
+            pltpu.VMEM((ROWS, 3 * D), BF),
+            pltpu.VMEM((ROWS, D), BF),
+            pltpu.VMEM((D, ROWS), BF),
+            pltpu.VMEM((D, ROWS), BF),
+            pltpu.VMEM((ROWS, D), F32),
+            pltpu.VMEM((ROWS, D), BF),
+            pltpu.VMEM((D, ROWS), BF),
+            pltpu.VMEM((ROWS, D), BF),
+            pltpu.VMEM((D, ROWS), BF),
+            pltpu.VMEM((ROWS, D), F32),
+            pltpu.VMEM((ROWS, D), F32),
+            pltpu.VMEM((ROWS, D), BF),
+            pltpu.VMEM((ROWS, D), BF),
+            pltpu.VMEM((2, 2, 2, 2, 8, 48, SB), BF),
+            pltpu.VMEM((ROWS, D), BF),
+            pltpu.SemaphoreType.DMA((NPIECE, 5)),
+            pltpu.SemaphoreType.DMA((NPIECE, 5)),
+            pltpu.SemaphoreType.DMA((NPIECE,)),
+            pltpu.SemaphoreType.DMA((8,)),
+            pltpu.SemaphoreType.DMA((2, 2, 2)),
+        ],
+        compiler_params=pltpu.CompilerParams(
+            collective_id=1, has_side_effects=True, vmem_limit_bytes=64 << 20
+        ),
+    )(gates, tokens, cot, segcol, segrow, hgate, ugate, mgate, gain, bias, qkv, out, up, down)
+
+
+def fast_body(
+    tokens,
+    segments,
+    head_mask,
+    unit_mask,
+    hidden_mask,
+    layer_gates,
+    qkv_weight,
+    out_weight,
+    norm_gain,
+    norm_bias,
+    up_weight,
+    down_weight,
+    cotangent,
+    owner_slot,
+    master,
+    left_stats,
+    right_stats,
+    left_root,
+    right_root,
+):
+    segcol = segments[:, :, None]
+    segrow = segments[:, None, :]
+    head_lanes = jnp.repeat(head_mask.astype(F32), HD)
+    hgate = head_lanes[None]
+    ugate = unit_mask.astype(F32).reshape(4, 1, D)
+    mgate = hidden_mask.astype(F32)[None]
+    (output, joined, ctx, ctxT, tokT, summed_grad, ff_grad, wq, wo, lse, small) = run_forward(
+        layer_gates,
+        tokens,
+        cotangent,
+        segcol,
+        segrow,
+        hgate,
+        ugate,
+        mgate,
+        norm_gain[None],
+        norm_bias[None],
+        qkv_weight,
+        out_weight,
+        up_weight,
+        down_weight,
+    )
+    factor = 1.0 / math.sqrt(HD)
+    qkv_full = wq.reshape(D, 3 * D)
+    out_full = wo.reshape(D, D)
+    out_back = (layer_gates[0] * summed_grad).astype(BF)
+    gated_grad = contract_cols(out_back, out_full).astype(BF)
+    head_row = jnp.sum(ctx.astype(F32) * gated_grad.astype(F32), axis=0)
+    context_grad = (gated_grad * hgate.astype(BF)).reshape(2, BLK, 12, HD)
+    log_totals = lse.reshape(2, 12, BLK) * math.log(2.0)
+    joined_grad = jax.vmap(partial(attend_backward, head_count=12, factor=factor))(
+        (joined.reshape(2, BLK, 3 * D), log_totals, context_grad, segments)
+    ).reshape(ROWS, 3 * D)
+    input_grad = summed_grad + contract_cols(joined_grad, qkv_full)
+    qkv_term = jnp.dot(tokT, joined_grad, preferred_element_type=F32).astype(BF)
+    out_term = jnp.dot(ctxT, out_back, preferred_element_type=F32) * head_lanes[:, None]
+    out_term = out_term.astype(BF)
+    tile = lambda v: v.reshape(2, SB, -1, SB).transpose(0, 2, 1, 3).reshape(-1, SB, SB)
+    blocks = jnp.concatenate([tile(qkv_term), tile(out_term), ff_grad.reshape(32, SB, SB)], axis=0)
+    small = small.at[9].set(head_row)
+    rows = lax.psum_scatter(
+        blocks.reshape(48, 4, 96, SB), "mp", scatter_dimension=1, tiled=True
+    ).reshape(48, 96, SB)
+    pick = (owner_slot[None, :] == jnp.arange(48)[:, None]).astype(BF)
+    slotted = jnp.dot(pick, rows.reshape(48, -1), preferred_element_type=F32).astype(BF)
+    owned = lax.psum_scatter(
+        slotted.reshape(48, 96, SB), "dp", scatter_dimension=0, tiled=True
+    )
+    full_grad = lax.all_gather(owned, "mp", axis=1, tiled=True).astype(F32)
+    owned = owned.astype(F32)
+    columns = lax.dynamic_slice_in_dim(full_grad, lax.axis_index("mp") * 96, 96, 2)
+    left_new = BETA * left_stats + (1.0 - BETA) * jnp.einsum(
+        "srj,skj->srk", owned, full_grad, precision=HIGH
+    )
+    right_new = BETA * right_stats + (1.0 - BETA) * jnp.einsum(
+        "sjr,sjk->srk", columns, full_grad, precision=HIGH
+    )
+    left_part = jnp.einsum("sri,sij->srj", left_root, full_grad, precision=HIGH)
+    update = jnp.einsum("srj,sjk->srk", left_part, right_root, precision=HIGH)
+    weight_new = master - RATE * update
+    small = lax.psum(small, ("dp", "mp"))
+    unit_grad = small[:4].reshape(-1)
+    norm_grad = small[4:6]
+    mask_grad = small[6]
+    layer_grad = jnp.sum(small[7:9], axis=1)
+    head_grad = jnp.sum(small[9].reshape(12, HD), axis=1)
+    norm_new = jnp.stack([norm_gain, norm_bias]) - 0.2 / math.sqrt(ROWS * 32) * norm_grad
+    return (
+        output,
+        input_grad,
+        head_grad,
+        unit_grad,
+        mask_grad,
+        layer_grad,
+        norm_grad,
+        norm_new,
+        owned,
+        left_new,
+        right_new,
+        weight_new,
+        weight_new.astype(BF),
+    )
+
+
 def solution(mesh):
     return jax.shard_map(
-        body,
+        fast_body if dict(mesh.shape) == {"dp": 8, "mp": 4} else body,
         mesh=mesh,
         in_specs=(
             P(("dp", "mp"), None),

time: 683 us -> 733 us (1.073)
  Pallas kernels: 0 us -> 120 us
  waiting for transfers between devices: 226 us -> 325 us
  matrix products: 187 us -> 94.4 us
  other arithmetic: 80.2 us -> 44.7 us
  local copies, waits for them, and re-layouts: 116 us -> 81.9 us
    unnamed x9 -> x4, waiting for transfers between devices: 106 us -> 245 us
    pallas_call x0 -> x1, Pallas kernels: none -> 120 us  [run_forward(): pl.pallas_call(forward_kernel, out_shape=outs, in_specs=[sm] + [vm] * 9 +...]
    dot_general x14 -> x7, matrix products: 114 us -> 18.5 us  [the longest x1 5.29 us: fast_body(): qkv_term = jnp.dot(tokT, joined_grad, preferred_element_type=F32).astype(BF)]
    all_gather x5 -> x1, waiting for transfers between devices: 39.9 us -> 0.01 us  [fast_body(): full_grad = lax.all_gather(owned, 'mp', axis=1, tiled=True).astype(F32)]
    while x29 -> x0, local copies, waits for them, and re-layouts: 29.6 us -> none  [the longest x3 18.1 us: body(): lax.map(partial(attend_backward, head_count=head_count, factor=factor), (...]
    dot_general x4 -> x2, matrix products: 35.9 us -> 15.4 us  [contract_cols(): lax.dot_general(left, right, (((1,), (1,)), ((), ())), preferred_element_...]
    convert_element_type x7 -> x6, other arithmetic: 26.4 us -> 7.04 us  [the longest x1 2.83 us: attend_backward(): return merged.reshape(merged.shape[0], -1).astype(jnp.bfloat16)]
    reduce_sum x6 -> x2, other arithmetic: 16.2 us -> 1.13 us  [the longest x1 0.63 us: fast_body(): head_grad = jnp.sum(small[9].reshape(12, HD), axis=1)]
  transfers between devices with their start and end apart: 9 -> 3, of which waited for: 4 -> 2; matrix products, arithmetic and copies ran while one was open for 39% -> 2% of each run, Pallas kernels for 0% -> 0%
where the time goes in v1:
time: 733 us; the launch traced here: 720 us
  waiting for transfers between devices  325 us (44%)
  Pallas kernels  120 us (16%)
  matrix products  94.4 us (13%)
  local copies, waits for them, and re-layouts  81.9 us (11%)
  other arithmetic  44.7 us (6%)
  blocking collectives  39 us (5%)
  between operations  14.2 us (2%)
    unnamed x4, waiting for transfers between devices  245 us
    pallas_call x1, Pallas kernels, run_forward(): pl.pallas_call(forward_kernel, out_shape=outs, in_specs=[sm] + [vm] * 9 +...  120 us
    reduce_scatter x1, waiting for transfers between devices, fast_body(): lax.psum_scatter(slotted.reshape(48, 96, SB), 'dp', scatter_dimension=0,...  79.5 us
    psum x1, blocking collectives, fast_body(): small = lax.psum(small, ('dp', 'mp'))  39 us
    convert_element_type x1, other arithmetic, attend_backward(): (weights_full * (weights_grad - inner_sum)).astype(jnp.bfloat16)  21.3 us
    dot_general x1, matrix products, attend_backward(): jnp.einsum('qhd,khd->hqk', context_grad, values_in, preferred_element_typ...  21 us
    dot_general x2, matrix products, contract_cols(): lax.dot_general(left, right, (((1,), (1,)), ((), ())), preferred_element_...  15.4 us
    unnamed x58, local copies, waits for them, and re-layouts  15 us
  transfers between devices with their start and end apart: 3, of which 2 were waited for; matrix products, arithmetic and copies ran while one was open for 2% of the time, Pallas kernels for 0%

profile of v1, /device:TPU:9, one launch (start us, length us, event | category | flops | bytes accessed | tf_op | source)
XLA Modules:
  0.0 719.6 jit_solution(4498773410350020938)
XLA Ops:
  19.3 120.4 %shard_map.282 = (bf16[1024,768]{1,0:T(8,128)(2,1)}, bf16[1024,2304]{1,0:T(8,128)(2,1)}, bf16[1024,768]{1,0:T(8,128)(2,1)}, bf16[768,1024]{1,0:T(8,128)(2,1)}, b...) custom-call(f32[2]{0:T(128)} %gates.1, ...), custom_call_target="tpu_custom_call" | custom-call | tf_op jit(solution)/shard_map/pallas_call | solution.py:709
  140.6 5.5 broadcast_multiply_fusion
  146.9 2.4 reshape.121
  149.3 6.7 copy.75
  156.0 8.8 %reshape_reshape.6 = bf16[2,512,3,12,64]{1,0,4,3,2:T(2,128)(2,1)} reshape(bf16[1024,2304]{0,1:T(8,128)(2,1)} %copy.75) | data formatting | bytes 9437184 | tf_op jit(solution)/shard_map/vmap()/reshape;reshape | solution.py:33
  164.8 6.3 fusion.19
  171.2 10.1 %fusion.8 = f32[2,12,512,512]{2,3,1,0:T(8,128)} fusion(bf16[2,512,1,12,64]{1,0,4,3,2:T(2,128)(2,1)S(1)} %get-tuple-element.53, bf16[2,512,1,12,64]{1,0,4,3,2:T(2,128)(2,1)S(1)} %get-tuple-element.52), kind=kOutput, calls=%fused_computation.22 | convolution fusion | flops 805306368 | bytes 28311552 | tf_op jit(solution)/shard_map/vmap(qhd,khd->hqk)/dot_general | solution.py:39
  181.2 12.9 %fusion.4 = bf16[2,512,12,64]{1,3,2,0:T(8,128)(2,1)} fusion(f32[2,12,512,512]{2,3,1,0:T(8,128)} %fusion.8, f32[2,12,512]{2,1,0:T(8,128)S(1)} %mul.86, pred[2,512,512]{1,2,0:T(8,128)(4,1)S(1)} %copy-done.4, bf16[2,512,12,64]{1,0,3,2:T(2,128)(2,1)S(1)} %copy-done.1), kind=kOutput, calls=%fused_computation.15 | convolution fusion | flops 830472192 | bytes 28884992 | tf_op jit(solution)/shard_map/vmap(hqk,qhd->khd)/dot_general | solution.py:63
  194.2 21.0 %multiply_reduce_fusion = (f32[2,12,512]{2,1,0:T(8,128)S(1)}, f32[2,12,512,512]{2,3,1,0:T(8,128)}) fusion(f32[2,12,512,512]{2,3,1,0:T(8,128)} %fusion.8, f32[2,12,512]{2,1,0:T(8,128)S(1)} %mul.86, pred[2,512,512]{1,2,0:T(8,128)(4,1)} %broadcast_compare_fusion, bf16[2,512,1,12,64]{1,0,4,3,2:T(2,128)(2,1)} %get-tuple-element.51, ...), kind=kOutput, calls=%fused_computation.2 | convolution fusion | flops 836751360 | bytes 54099968 | tf_op jit(solution)/shard_map/vmap(qhd,khd->hqk)/dot_general | solution.py:66
  215.2 21.3 %multiply_convert_fusion = bf16[2,12,512,512]{2,3,1,0:T(8,128)(2,1)} fusion(f32[2,12,512,512]{2,3,1,0:T(8,128)} %get-tuple-element.58, f32[2,12,512,512]{2,3,1,0:T(8,128)} %fusion.8, f32[2,12,512]{2,1,0:T(8,128)S(1)} %get-tuple-element.57, f32[2,12,512]{2,1,0:T(8,128)S(1)} %mul.86, pred[2,512,512]{1,2,0:T(8,128)(4,1)} %broadcast_compare_fusion), kind=kLoop, calls=%fused_computation.1 | loop fusion | flops 37748736 | bytes 63537152 | tf_op jit(solution)/shard_map/vmap()/convert_element_type | solution.py:70
  236.5 9.6 %multiply_bitcast_fusion = bf16[2,512,12,64]{1,3,2,0:T(8,128)(2,1)} fusion(bf16[2,12,512,512]{2,3,1,0:T(8,128)(2,1)} %multiply_convert_fusion, bf16[2,512,1,12,64]{1,0,4,3,2:T(2,128)(2,1)S(1)} %get-tuple-element.52), kind=kOutput, calls=%fused_computation.11 | convolution fusion | flops 806879232 | bytes 15728640 | tf_op jit(solution)/shard_map/vmap(hqk,qhd->khd)/dot_general | solution.py:76
  246.1 6.9 multiply_bitcast_fusion.1
  253.0 2.5 multiply_convert_fusion.2
  255.5 3.7 reshape.126
  259.2 2.5 copy.88
  261.7 2.8 maximum_convert_fusion
  264.6 9.4 %copy.85 = bf16[2,512,36,64]{1,0,3,2:T(2,128)(2,1)} copy(bf16[2,512,36,64]{1,3,2,0:T(8,128)(2,1)} %maximum_convert_fusion) | data formatting | bytes 9437184 | tf_op jit(solution)/shard_map/vmap()/convert_element_type | solution.py:80
  274.0 4.0 copy.100
  278.0 2.1 copy-done.5
  280.1 5.3 convolution_convert_fusion.1
  285.4 4.5 copy.86
  289.9 3.1 reshape.125
  293.0 10.4 %copy.87 = bf16[2,6,384,384]{3,2,1,0:T(8,128)(2,1)S(1)} copy(bf16[2,6,384,384]{2,0,3,1:T(2,128)(2,1)} %bitcast.75) | data formatting | bytes 7077888 | tf_op jit(solution)/shard_map/transpose | solution.py:804
  303.4 11.1 %pad_maximum_fusion = bf16[48,4,96,384]{3,2,1,0:T(8,128)(2,1)} fusion(bf16[32,4,96,384]{3,2,1,0:T(8,128)(2,1)} %bitcast.76, bf16[4,4,96,384]{3,2,1,0:T(8,128)(2,1)} %bitcast.77, bf16[12,4,96,384]{3,2,1,0:T(8,128)(2,1)S(1)} %bitcast.74), kind=kLoop, calls=%fused_computation.4 | loop fusion | flops 14155776 | bytes 28311552 | tf_op jit(solution)/shard_map/concatenate | solution.py:805
  315.7 245.2 %all-reduce.3.cloned.1.call-done = bf16[48,4,96,384]{3,2,1,0:T(8,128)(2,1)} async-done(((bf16[48,4,96,384]{3,2,1,0:T(8,128)(2,1)}), bf16[48,4,96,384]{3,2,1,0:T(8,128)(2,1)}) %all-reduce.3.cloned.1.call-update) | async-done | bytes 14155792
  560.9 3.0 constant_dynamic-slice_fusion
  566.4 2.3 copy.102
  568.8 79.5 %reduce-scatter.5.cloned.1.call-done = bf16[6,96,384]{2,1,0:T(8,128)(2,1)} async-done(((bf16[48,96,384]{2,1,0:T(8,128)(2,1)}), bf16[6,96,384]{2,1,0:T(8,128)(2,1)}) %reduce-scatter.5.cloned.1.call-update) | async-done | bytes 442384 | tf_op jit(solution)/shard_map/reduce_scatter | solution.py:812
  648.9 39.0 %psum.7 = f32[16,768]{1,0:T(8,128)S(1)} all-reduce(f32[16,768]{1,0:T(8,128)S(1)} %scatter.4), channel_id=1, replica_groups=mesh['dp'=8,'mp'=4] {'dp','mp'}, use_global_device_ids=true, to_apply=%region_2.3 | all-reduce | flops 12288 | bytes 98304 | tf_op jit(solution)/shard_map/psum | solution.py:827
  691.1 10.0 %convolution_add_fusion = f32[1024,768]{1,0:T(8,128)} fusion(f32[1024,768]{1,0:T(8,128)} %get-tuple-element.37, bf16[1024,2304]{0,1:T(8,128)(2,1)} %bitcast.79, bf16[768,2304]{1,0:T(8,128)(2,1)} %bitcast.86), kind=kOutput, calls=%fused_computation.16 | convolution fusion | flops 3624665088 | bytes 14548992 | tf_op jit(solution)/shard_map/dot_general | solution.py:90
  702.0 2.8 fusion.21
  704.8 3.5 fusion.20
  (90 shorter events, 26.9 us)
Async XLA Ops:
  7.2 553.7 %all-reduce.3.cloned.1.call-start = ((), (), s32[]{:S(2)}) async-start(), calls=%async_computation.3 | async-start | bytes 28311552
  8.7 7.0 copy-start.19
  171.2 10.1 %copy-start.1 = (bf16[2,512,12,64]{1,0,3,2:T(2,128)(2,1)S(1)}, bf16[2,512,12,64]{1,0,3,2:T(2,128)(2,1)}, u32[]{:S(2)}) copy-start(bf16[2,512,12,64]{1,0,3,2:T(2,128)(2,1)} %reshape.121) | copy-start | bytes 4718596
  171.2 10.1 %copy-start.4 = (pred[2,512,512]{1,2,0:T(8,128)(4,1)S(1)}, pred[2,512,512]{1,2,0:T(8,128)(4,1)}, u32[]{:S(2)}) copy-start(pred[2,512,512]{1,2,0:T(8,128)(4,1)} %broadcast_compare_fusion) | copy-start | bytes 1572868
  246.1 6.9 copy-start.8
  246.1 6.9 copy-start.20
  246.1 6.9 copy-start.21
  246.1 6.9 copy-start.24
  255.5 6.2 copy-start.3
  259.2 2.6 copy-start.9
  274.0 6.1 copy-start.23
  278.0 2.1 copy-start.5
  314.5 0.7 copy-start.25
  314.5 333.7 %reduce-scatter.5.cloned.1.call-start = ((), (), s32[]{:S(2)}) async-start(), calls=%async_computation.1 | async-start | bytes 3981312 | tf_op jit(solution)/shard_map/reduce_scatter | solution.py:812
  563.9 1.4 copy-start.22
  568.7 79.6 %copy-start.2 = (bf16[1024,768]{1,0:T(8,128)(2,1)S(1)}, bf16[1024,768]{1,0:T(8,128)(2,1)}, u32[]{:S(2)}) copy-start(bf16[1024,768]{1,0:T(8,128)(2,1)} %get-tuple-element.56) | copy-start | bytes 4718596
  568.7 79.6 %copy-start.11 = (bf16[1024,768]{1,0:T(8,128)(2,1)S(1)}, bf16[1024,768]{1,0:T(8,128)(2,1)}, u32[]{:S(2)}) copy-start(bf16[1024,768]{1,0:T(8,128)(2,1)} %get-tuple-element.43) | copy-start | bytes 4718596
  568.7 80.1 %copy-start.16 = (f32[16,768]{1,0:T(8,128)S(1)}, f32[16,768]{1,0:T(8,128)}, u32[]{:S(2)}) copy-start(f32[16,768]{1,0:T(8,128)} %get-tuple-element.42) | copy-start | bytes 147460
  568.7 121.1 %copy-start.17 = (f32[1,768]{1,0:T(1,128)S(1)}, f32[1,768]{1,0:T(1,128)}, u32[]{:S(2)}) copy-start(f32[1,768]{1,0:T(1,128)} %broadcast_in_dim.41.gain) | copy-start | bytes 9220
  568.7 121.1 %copy-start.18 = (f32[1,768]{1,0:T(1,128)S(1)}, f32[1,768]{1,0:T(1,128)}, u32[]{:S(2)}) copy-start(f32[1,768]{1,0:T(1,128)} %broadcast_in_dim.42.bias) | copy-start | bytes 9220
  568.8 133.2 %all-gather.2.cloned.1.call-start = ((), (), s32[]{:S(2)}) async-start(), calls=%async_computation.2 | async-start | bytes 2211840 | tf_op jit(solution)/shard_map/all_gather | solution.py:815
  691.1 10.0 %copy-start.6 = (bf16[6,96,384]{2,1,0:T(8,128)(2,1)S(1)}, bf16[6,96,384]{2,1,0:T(8,128)(2,1)}, u32[]{:S(2)}) copy-start(bf16[6,96,384]{2,1,0:T(8,128)(2,1)} %reduce-scatter.5.cloned.1.call-done) | copy-start | bytes 1327108
  691.1 10.9 %copy-start.12 = (f32[6,96,384]{2,1,0:T(8,128)S(1)}, f32[6,96,384]{2,1,0:T(8,128)}, u32[]{:S(2)}) copy-start(f32[6,96,384]{2,1,0:T(8,128)} %param.38) | copy-start | bytes 2654212
  701.0 3.8 copy-start.13
  702.0 2.8 copy-start.7
  704.8 3.5 copy-start
  704.8 3.5 copy-start.14
  708.3 1.6 copy-start.15
  708.3 3.4 copy-start.10
Sparse Core Ops, SparseCore 0:
  314.6 246.2 all-reduce.2
  568.9 79.3 reduce-scatter.4
  649.8 20.9 all-gather.1

commit v2 on v1

--- a/solution.py
+++ b/solution.py
@@ -743,6 +743,521 @@
     )(gates, tokens, cot, segcol, segrow, hgate, ugate, mgate, gain, bias, qkv, out, up, down)
 
 
+SENT = (12, 13, 14, 15, 0, 2, 4, 6, 8, 10, 1, 3, 5, 7, 9, 11)
+GROUPS = ((0, 8), (8, 8), (16, 8), (24, 8), (32, 10), (42, 6))
+FF_BLOCKS = 32
+
+
+def backward_kernel(
+    gates,
+    order,
+    small_in,
+    hgate,
+    hcol,
+    segcol,
+    segrow,
+    lse,
+    g_in,
+    joined_in,
+    ctx_in,
+    ctxT_in,
+    tokT_in,
+    sgrad_in,
+    wq_in,
+    wo_in,
+    o_igrad,
+    o_full,
+    small_out,
+    joined,
+    ctx,
+    ctxT,
+    tokT,
+    sgrad,
+    wq,
+    wo,
+    outb,
+    cgrad,
+    igrad,
+    half,
+    ga,
+    got1,
+    got2,
+    got3,
+    part,
+    slots,
+    gotz,
+    gz,
+    gfull,
+    sm,
+    gots,
+    load_sem,
+    half_sem,
+    send_sem,
+    recv_sem,
+    z_send,
+    z_recv,
+    f_send,
+    f_recv,
+    s_send,
+    s_recv,
+    out_sem,
+):
+    z, x, y, c = coords()
+    g0 = gates[0]
+    sib = at(z, x, y, 1 - c)
+    ypeer = at(z, x, 1 - y, c)
+    xpeer = at(z, 1 - x, y, c)
+    diag = at(z, 1 - x, 1 - y, c)
+    zpeers = [at((z + k) % 4, x, y, c) for k in (1, 2, 3)]
+
+    loads = [
+        pltpu.make_async_copy(src, dst, load_sem.at[i])
+        for i, (src, dst) in enumerate(
+            (
+                (sgrad_in, sgrad),
+                (wo_in, wo),
+                (ctx_in, ctx),
+                (ctxT_in, ctxT),
+                (joined_in, joined),
+                (tokT_in, tokT),
+                (wq_in, wq),
+            )
+        )
+    ]
+    halves_in = [
+        pltpu.make_async_copy(
+            g_in.at[pl.ds(8 * g, 8), c], half.at[pl.ds(8 * g, 8)], half_sem.at[g]
+        )
+        for g in range(4)
+    ]
+    for copy in loads[:4]:
+        copy.start()
+
+    barrier = pltpu.get_barrier_semaphore()
+    for peer in [sib, ypeer, xpeer, diag] + zpeers:
+        pl.semaphore_signal(barrier, inc=1, device_id=peer, device_id_type=MESH)
+    pl.semaphore_wait(barrier, 7)
+
+    def remote(src, dst, sems, dev):
+        return pltpu.make_async_remote_copy(
+            src_ref=src,
+            dst_ref=dst,
+            send_sem=sems[0],
+            recv_sem=sems[1],
+            device_id=dev,
+            device_id_type=MESH,
+        )
+
+    def pair(g, k):
+        return send_sem.at[g, k], recv_sem.at[g, k]
+
+    def block(n):
+        def ref(i):
+            return half.at[i] if n < FF_BLOCKS else ga.at[i - FF_BLOCKS, c]
+
+        return ref
+
+    def mine(g, first, count):
+        base = GROUPS[g][0] + first
+        if base < FF_BLOCKS:
+            return half.at[pl.ds(base, count)]
+        return ga.at[pl.ds(base - FF_BLOCKS, count), c]
+
+    def swap1(g):
+        base, count = GROUPS[g]
+        if base < FF_BLOCKS:
+            src = g_in.at[pl.ds(base, count), 1 - c]
+        else:
+            src = ga.at[pl.ds(base - FF_BLOCKS, count), 1 - c]
+        return remote(src, got1.at[pl.ds(base, count)], pair(g, 0), sib)
+
+    def swap2(g):
+        base, count = GROUPS[g]
+        n = count // 2
+        return (
+            remote(mine(g, 0, n).at[:, 1 - y], got2.at[pl.ds(base, n)], pair(g, 1), ypeer),
+            remote(
+                mine(g, n, n).at[:, :, 1 - x], got2.at[pl.ds(base + n, n)], pair(g, 2), xpeer
+            ),
+        )
+
+    def swap3(g):
+        base, count = GROUPS[g]
+        n = count // 2
+        return (
+            remote(mine(g, 0, n).at[:, y, 1 - x], got3.at[pl.ds(base, n)], pair(g, 3), xpeer),
+            remote(
+                mine(g, n, n).at[:, 1 - y, x], got3.at[pl.ds(base + n, n)], pair(g, 4), ypeer
+            ),
+        )
+
+    def plus(left, right):
+        return (left.astype(F32) + right.astype(F32)).astype(BF)
+
+    def step1(g):
+        base, count = GROUPS[g]
+        if g < 4:
+            halves_in[g].wait()
+        swap1(g).wait_recv()
+
+        @pl.loop(base, base + count)
+        def _(i):
+            ref = block(base)(i)
+            ref[...] = plus(ref[...], got1[i])
+
+        for copy in swap2(g):
+            copy.start()
+
+    def step2(g):
+        base, count = GROUPS[g]
+        n = count // 2
+        for copy in swap2(g):
+            copy.wait_recv()
+
+        @pl.loop(base, base + n)
+        def _(i):
+            ref = block(base)(i)
+            ref[y] = plus(ref[y], got2[i])
+
+        @pl.loop(base + n, base + count)
+        def _(i):
+            ref = block(base)(i)
+            ref[0, x] = plus(ref[0, x], got2[i, 0])
+            ref[1, x] = plus(ref[1, x], got2[i, 1])
+
+        for copy in swap3(g):
+            copy.start()
+
+    def step3(g):
+        base, count = GROUPS[g]
+        for copy in swap3(g):
+            copy.wait_recv()
+
+        @pl.loop(base, base + count)
+        def _(i):
+            part[i] = plus(block(base)(i)[y, x], got3[i])
+
+    small_peers = [sib, ypeer, xpeer] + zpeers
+
+    def small_copy(k):
+        return remote(sm.at[min(k, 3)], gots.at[k], (s_send.at[k], s_recv.at[k]), small_peers[k])
+
+    def small_step(k):
+        small_copy(k).wait_recv()
+        if k < 3:
+            sm[k + 1] = sm[k] + gots[k]
+            if k < 2:
+                small_copy(k + 1).start()
+            else:
+                for j in (3, 4, 5):
+                    small_copy(j).start()
+        else:
+            small_copy(4).wait_recv()
+            small_copy(5).wait_recv()
+            small_out[...] = sm[3] + gots[3] + gots[4] + gots[5]
+
+    for g in range(4):
+        swap1(g).start()
+        halves_in[g].start()
+    for copy in loads[4:]:
+        copy.start()
+
+    loads[0].wait()
+    loads[1].wait()
+    loads[2].wait()
+    sm[0] = small_in[...]
+
+    @pl.loop(0, 4)
+    def _(r):
+        rows = pl.ds(pl.multiple_of(r * 256, 256), 256)
+        low = (g0 * sgrad[rows, :]).astype(BF)
+        outb[rows, :] = low
+        grad = nt(low, wo[...].reshape(D, D)).astype(BF)
+        sm[0, 9:10, :] += colsum(ctx[rows, :].astype(F32) * grad.astype(F32))
+        cgrad[rows, :] = grad * hgate[...].astype(BF)
+
+    small_copy(0).start()
+    loads[3].wait()
+
+    def weight_tiles(left, right, lane, rowgate, places):
+        @pl.loop(0, 8)
+        def _(t):
+            rr = pl.ds(pl.multiple_of(t * 96, 16), 96)
+            g = nn(left[rr, :], right[:, pl.ds(lane, SB)])
+            if rowgate is not None:
+                g = g * rowgate[rr, :]
+            g = g.astype(BF)
+            to = places[0] + (t // 4) * (places[1] - places[0])
+            u = t % 4
+            for h in range(2):
+                ga[to, u // 2, u % 2, h] = g[48 * h : 48 * h + 48]
+
+    for j in range(2):
+        weight_tiles(ctxT, outb, SB * j, hcol, (SENT.index(12 + j), SENT.index(14 + j)))
+
+    step1(0)
+    step1(1)
+    step1(2)
+    step1(3)
+    loads[4].wait()
+
+    scale = LOG2E / math.sqrt(HD)
+    factor = 1.0 / math.sqrt(HD)
+    half_iota = lax.broadcasted_iota(jnp.int32, (1, 128), 1) // HD
+    halves = [(half_iota == e).astype(F32).astype(BF) for e in range(2)]
+
+    def attend_back(i):
+        p = i // 2
+        b = i % 2
+        rows = pl.ds(pl.multiple_of(b * BLK, BLK), BLK)
+        lane = pl.multiple_of(p * 128, 128)
+        q = joined[rows, pl.ds(lane, 128)]
+        k = joined[rows, pl.ds(D + lane, 128)]
+        v = joined[rows, pl.ds(2 * D + lane, 128)]
+        do = cgrad[rows, pl.ds(lane, 128)]
+        sc = segcol[b]
+        sr = segrow[b]
+        dv = None
+        dk = None
+        for qt in range(2):
+            cols = slice(qt * 256, qt * 256 + 256)
+            allowed = sc == sr[:, cols]
+            dqT = None
+            for e in range(2):
+                ke = k * halves[e]
+                s = nt(ke, q[cols])
+                s = jnp.where(allowed, s * scale, MASKED)
+                pr = jnp.exp2(s - lse[2 * (b * 6 + p) + e, :, pl.ds(qt * 256, 256)])
+                dp = nt(v * halves[e], do[cols])
+                delta = jnp.sum(pr * dp, axis=0, keepdims=True)
+                ds = (pr * (dp - delta)).astype(BF)
+                dv_part = nn(pr.astype(BF), do[cols] * halves[e])
+                dk_part = nn(ds, q[cols] * halves[e])
+                dq_part = nn(ke.T, ds)
+                dv = dv_part if dv is None else dv + dv_part
+                dk = dk_part if dk is None else dk + dk_part
+                dqT = dq_part if dqT is None else dqT + dq_part
+            qrows = pl.ds(pl.multiple_of(b * BLK + qt * 256, 256), 256)
+            joined[qrows, pl.ds(lane, 128)] = (dqT * factor).T.astype(BF)
+        joined[rows, pl.ds(D + lane, 128)] = (dk * factor).astype(BF)
+        joined[rows, pl.ds(2 * D + lane, 128)] = dv.astype(BF)
+
+    def qkv_tiles(h):
+        for j in (h, 2 + h, 4 + h):
+            weight_tiles(tokT, joined, SB * j, None, (SENT.index(j), SENT.index(6 + j)))
+
+    def middle():
+        loads[5].wait()
+        qkv_tiles(0)
+        swap1(4).start()
+
+    plan = {
+        0: [lambda: small_step(0)],
+        1: [lambda: step2(0), lambda: small_step(1)],
+        2: [lambda: small_step(2)],
+        3: [lambda: step2(1), lambda: small_step(3)],
+        5: [lambda: step2(2), middle],
+        6: [lambda: step1(4), lambda: step3(0)],
+        7: [lambda: step2(3), lambda: step3(1)],
+        8: [lambda: step3(2)],
+        10: [lambda: step2(4), lambda: step3(3)],
+    }
+
+    @pl.loop(0, 12)
+    def _(i):
+        attend_back(i)
+        for at_step, todo in plan.items():
+
+            @pl.when(i == at_step)
+            def _(todo=todo):
+                for f in todo:
+                    f()
+
+    qkv_tiles(1)
+    swap1(5).start()
+    loads[6].wait()
+
+    def input_rows(lo, hi):
+        @pl.loop(lo, hi)
+        def _(r):
+            rows = pl.ds(pl.multiple_of(r * 128, 128), 128)
+            igrad[rows, :] = sgrad[rows, :] + nt(joined[rows, :], wq[...].reshape(D, 3 * D))
+
+    input_rows(0, 2)
+    step1(5)
+    step3(4)
+    input_rows(2, 6)
+    step2(5)
+    input_rows(6, 8)
+    igrad_copy = pltpu.make_async_copy(igrad, o_igrad, out_sem.at[0])
+    igrad_copy.start()
+    step3(5)
+
+    @pl.loop(0, 48)
+    def _(s):
+        slots[s] = part[order[s]]
+
+    z_copies = []
+    for k in (1, 2, 3):
+        other = (z + k) % 4
+        z_copies.append(
+            remote(
+                slots.at[pl.ds(12 * other, 12)],
+                gotz.at[k - 1],
+                (z_send.at[k - 1], z_recv.at[k - 1]),
+                zpeers[k - 1],
+            )
+        )
+    for copy in z_copies:
+        copy.start()
+    for copy in z_copies:
+        copy.wait_recv()
+
+    @pl.loop(0, 12)
+    def _(s):
+        total = slots[12 * z + s].astype(F32)
+        for k in range(3):
+            total = total + gotz[k, s].astype(F32)
+        gz[s] = total.astype(BF)
+
+    def piece(cc, yy, xx):
+        return gfull.at[:, 4 * cc + 2 * yy + xx]
+
+    here = gz.at[pl.ds(6 * x, 6)]
+    there = gz.at[pl.ds(6 * (1 - x), 6)]
+
+    def fsem(k):
+        return f_send.at[k], f_recv.at[k]
+
+    near = [
+        remote(there, piece(c, y, x), fsem(0), xpeer),
+        remote(here, piece(c, y, x), fsem(1), ypeer),
+        remote(there, piece(c, y, x), fsem(2), diag),
+        remote(here, piece(c, y, x), fsem(3), sib),
+    ]
+    for copy in near:
+        copy.start()
+    own_copy = pltpu.make_async_copy(here, piece(c, y, x), out_sem.at[1])
+    own_copy.start()
+    onward = []
+    for k, (yy, xx) in enumerate(((y, 1 - x), (1 - y, x), (1 - y, 1 - x))):
+        near[k].wait_recv()
+        copy = remote(piece(c, yy, xx), piece(c, yy, xx), fsem(4 + k), sib)
+        copy.start()
+        onward.append(copy)
+    near[3].wait_recv()
+    for copy in onward:
+        copy.wait_recv()
+    own_copy.wait()
+    full_copy = pltpu.make_async_copy(gfull, o_full, out_sem.at[2])
+    full_copy.start()
+    for copy in near + onward + z_copies:
+        copy.wait_send()
+    for k in range(6):
+        small_copy(k).wait_send()
+    for g in range(len(GROUPS)):
+        for copy in (swap1(g),) + swap2(g) + swap3(g):
+            copy.wait_send()
+    igrad_copy.wait()
+    full_copy.wait()
+
+
+def run_backward(gates, order, small, hgate, hcol, segcol, segrow, lse, *arrays):
+    sds = jax.ShapeDtypeStruct
+    outs = (sds((ROWS, D), F32), sds((6, 8, 48, SB), BF), sds((16, D), F32))
+    any_ = pl.BlockSpec(memory_space=pl.ANY)
+    vm = pl.BlockSpec(memory_space=pltpu.VMEM)
+    sm = pl.BlockSpec(memory_space=pltpu.SMEM)
+    dma = pltpu.SemaphoreType.DMA
+    return pl.pallas_call(
+        backward_kernel,
+        out_shape=outs,
+        in_specs=[sm] * 2 + [vm] * 6 + [any_] * 8,
+        out_specs=[any_] * 2 + [vm],
+        scratch_shapes=[
+            pltpu.VMEM((ROWS, 3 * D), BF),
+            pltpu.VMEM((ROWS, D), BF),
+            pltpu.VMEM((D, ROWS), BF),
+            pltpu.VMEM((D, ROWS), BF),
+            pltpu.VMEM((ROWS, D), F32),
+            pltpu.VMEM((4, 192, 3 * D), BF),
+            pltpu.VMEM((4, 192, D), BF),
+            pltpu.VMEM((ROWS, D), BF),
+            pltpu.VMEM((ROWS, D), BF),
+            pltpu.VMEM((ROWS, D), F32),
+            pltpu.VMEM((32, 2, 2, 48, SB), BF),
+            pltpu.VMEM((16, 2, 2, 2, 48, SB), BF),
+            pltpu.VMEM((48, 2, 2, 48, SB), BF),
+            pltpu.VMEM((48, 2, 48, SB), BF),
+            pltpu.VMEM((48, 48, SB), BF),
+            pltpu.VMEM((48, 48, SB), BF),
+            pltpu.VMEM((48, 48, SB), BF),
+            pltpu.VMEM((3, 12, 48, SB), BF),
+            pltpu.VMEM((12, 48, SB), BF),
+            pltpu.VMEM((6, 8, 48, SB), BF),
+            pltpu.VMEM((4, 16, D), F32),
+            pltpu.VMEM((6, 16, D), F32),
+            dma((7,)),
+            dma((4,)),
+            dma((6, 5)),
+            dma((6, 5)),
+            dma((3,)),
+            dma((3,)),
+            dma((7,)),
+            dma((7,)),
+            dma((6,)),
+            dma((6,)),
+            dma((3,)),
+        ],
+        compiler_params=pltpu.CompilerParams(
+            collective_id=2, has_side_effects=True, vmem_limit_bytes=64 << 20
+        ),
+    )(gates, order, small, hgate, hcol, segcol, segrow, lse, *arrays)
+
+
+def split(value):
+    high = value.astype(BF)
+    return high, (value - high.astype(F32)).astype(BF)
+
+
+def update_kernel(
+    full, master, left_stats, right_stats, left_root, right_root, o_grad, o_left, o_right, o_new, o_copy, turned
+):
+    start = pl.multiple_of(lax.axis_index("mp") * 96, 16)
+    own = full[0, pl.ds(start, 96), :]
+    whole = full[0]
+    o_grad[0] = own.astype(F32)
+    o_left[0] = BETA * left_stats[0] + (1.0 - BETA) * nt(own, whole)
+    turned[...] = whole.T
+    o_right[0] = BETA * right_stats[0] + (1.0 - BETA) * nn(turned[pl.ds(start, 96), :], whole)
+    root_high, root_low = split(left_root[0])
+    left_part = nn(root_high, whole) + nn(root_low, whole)
+    part_high, part_low = split(left_part)
+    right_high, right_low = split(right_root[0])
+    update = nn(part_high, right_high) + nn(part_low, right_high) + nn(part_high, right_low)
+    new = master[0] - RATE * update
+    o_new[0] = new
+    o_copy[0] = new.astype(BF)
+
+
+def run_update(full, master, left_stats, right_stats, left_root, right_root):
+    sds = jax.ShapeDtypeStruct
+    whole = pl.BlockSpec((1, SB, SB), lambda s: (s, 0, 0))
+    rows = pl.BlockSpec((1, 96, SB), lambda s: (s, 0, 0))
+    return pl.pallas_call(
+        update_kernel,
+        grid=(6,),
+        out_shape=(sds((6, 96, SB), F32),) * 4 + (sds((6, 96, SB), BF),),
+        in_specs=[whole] + [rows] * 4 + [whole],
+        out_specs=[rows] * 5,
+        scratch_shapes=[pltpu.VMEM((SB, SB), BF)],
+        compiler_params=pltpu.CompilerParams(vmem_limit_bytes=32 << 20),
+    )(full, master, left_stats, right_stats, left_root, right_root)
+
+
+PLACE = tuple(FF_BLOCKS + SENT.index(b) for b in range(16)) + tuple(range(32))
+
+
 def fast_body(
     tokens,
     segments,
@@ -786,45 +1301,30 @@
         up_weight,
         down_weight,
     )
-    factor = 1.0 / math.sqrt(HD)
-    qkv_full = wq.reshape(D, 3 * D)
-    out_full = wo.reshape(D, D)
-    out_back = (layer_gates[0] * summed_grad).astype(BF)
-    gated_grad = contract_cols(out_back, out_full).astype(BF)
-    head_row = jnp.sum(ctx.astype(F32) * gated_grad.astype(F32), axis=0)
-    context_grad = (gated_grad * hgate.astype(BF)).reshape(2, BLK, 12, HD)
-    log_totals = lse.reshape(2, 12, BLK) * math.log(2.0)
-    joined_grad = jax.vmap(partial(attend_backward, head_count=12, factor=factor))(
-        (joined.reshape(2, BLK, 3 * D), log_totals, context_grad, segments)
-    ).reshape(ROWS, 3 * D)
-    input_grad = summed_grad + contract_cols(joined_grad, qkv_full)
-    qkv_term = jnp.dot(tokT, joined_grad, preferred_element_type=F32).astype(BF)
-    out_term = jnp.dot(ctxT, out_back, preferred_element_type=F32) * head_lanes[:, None]
-    out_term = out_term.astype(BF)
-    tile = lambda v: v.reshape(2, SB, -1, SB).transpose(0, 2, 1, 3).reshape(-1, SB, SB)
-    blocks = jnp.concatenate([tile(qkv_term), tile(out_term), ff_grad.reshape(32, SB, SB)], axis=0)
-    small = small.at[9].set(head_row)
-    rows = lax.psum_scatter(
-        blocks.reshape(48, 4, 96, SB), "mp", scatter_dimension=1, tiled=True
-    ).reshape(48, 96, SB)
-    pick = (owner_slot[None, :] == jnp.arange(48)[:, None]).astype(BF)
-    slotted = jnp.dot(pick, rows.reshape(48, -1), preferred_element_type=F32).astype(BF)
-    owned = lax.psum_scatter(
-        slotted.reshape(48, 96, SB), "dp", scatter_dimension=0, tiled=True
-    )
-    full_grad = lax.all_gather(owned, "mp", axis=1, tiled=True).astype(F32)
-    owned = owned.astype(F32)
-    columns = lax.dynamic_slice_in_dim(full_grad, lax.axis_index("mp") * 96, 96, 2)
-    left_new = BETA * left_stats + (1.0 - BETA) * jnp.einsum(
-        "srj,skj->srk", owned, full_grad, precision=HIGH
-    )
-    right_new = BETA * right_stats + (1.0 - BETA) * jnp.einsum(
-        "sjr,sjk->srk", columns, full_grad, precision=HIGH
-    )
-    left_part = jnp.einsum("sri,sij->srj", left_root, full_grad, precision=HIGH)
-    update = jnp.einsum("srj,sjk->srk", left_part, right_root, precision=HIGH)
-    weight_new = master - RATE * update
-    small = lax.psum(small, ("dp", "mp"))
+    slot_order = jnp.sum(
+        jnp.where(owner_slot[None, :] == jnp.arange(48)[:, None], jnp.asarray(PLACE)[None, :], 0), axis=1
+    )
+    input_grad, full, small = run_backward(
+        layer_gates,
+        slot_order,
+        small,
+        hgate,
+        head_lanes[:, None],
+        segcol,
+        segrow,
+        lse,
+        ff_grad.reshape(32, 2, 2, 2, 48, SB),
+        joined,
+        ctx,
+        ctxT,
+        tokT,
+        summed_grad,
+        wq,
+        wo,
+    )
+    owned, left_new, right_new, weight_new, weight_copy = run_update(
+        full.reshape(6, SB, SB), master, left_stats, right_stats, left_root, right_root
+    )
     unit_grad = small[:4].reshape(-1)
     norm_grad = small[4:6]
     mask_grad = small[6]
@@ -844,7 +1344,7 @@
         left_new,
         right_new,
         weight_new,
-        weight_new.astype(BF),
+        weight_copy,
     )
 
 

time: 733 us -> 313 us (0.43); the launches traced: 720 us -> 312 us
  waiting for transfers between devices: 325 us -> 0 us
  Pallas kernels: 120 us -> 281 us
  matrix products: 94.4 us -> 0 us
  local copies, waits for them, and re-layouts: 81.9 us -> 23 us
  blocking collectives: 39 us -> 0 us
  other arithmetic: 44.7 us -> 6.7 us
  between operations: 14.2 us -> 0.68 us
    unnamed x4 -> x0, waiting for transfers between devices: 245 us -> none
    pallas_call x0 -> x2, Pallas kernels: none -> 161 us  [the longest x1 156 us: run_backward(): pl.pallas_call(backward_kernel, out_shape=outs, in_specs=[sm] * 2 + [vm]...]
    dot_general x14 -> x0, matrix products: 94.4 us -> none  [the longest x1 21 us: attend_backward(): jnp.einsum('qhd,khd->hqk', context_grad, values_in, preferred_element_typ...]
    reduce_scatter x1 -> x0, waiting for transfers between devices: 79.5 us -> none  [fast_body(): lax.psum_scatter(slotted.reshape(48, 96, SB), 'dp', scatter_dimension=0,...]
    psum x1 -> x0, blocking collectives: 39 us -> none  [fast_body(): small = lax.psum(small, ('dp', 'mp'))]
    convert_element_type x4 -> x0, other arithmetic: 25.7 us -> none  [the longest x1 21.3 us: attend_backward(): (weights_full * (weights_grad - inner_sum)).astype(jnp.bfloat16)]
    convert_element_type x2 -> x0, local copies, waits for them, and re-layouts: 13.9 us -> none  [the longest x1 9.42 us: attend_backward(): return merged.reshape(merged.shape[0], -1).astype(jnp.bfloat16)]
    transpose x2 -> x0, local copies, waits for them, and re-layouts: 12.9 us -> none  [fast_body(): v.reshape(2, SB, -1, SB).transpose(0, 2, 1, 3).reshape(-1, SB, SB)]
  transfers between devices with their start and end apart: 3 -> 0, of which waited for: 2 -> 0; matrix products, arithmetic and copies ran while one was open for 2% -> 0% of each run, Pallas kernels for 0% -> 0%
where the time goes in v2:
time: 313 us; the launch traced here: 312 us
  Pallas kernels  281 us (90%)
  local copies, waits for them, and re-layouts  23 us (7%)
  other arithmetic  6.7 us (2%)
    pallas_call x1, Pallas kernels, run_backward(): pl.pallas_call(backward_kernel, out_shape=outs, in_specs=[sm] * 2 + [vm]...  156 us
    pallas_call x1, Pallas kernels, run_forward(): pl.pallas_call(forward_kernel, out_shape=outs, in_specs=[sm] + [vm] * 9 +...  120 us
    unnamed x18, local copies, waits for them, and re-layouts  12.3 us

profile of v2, /device:TPU:9, one launch (start us, length us, event | category | flops | bytes accessed | tf_op | source)
XLA Modules:
  0.0 311.8 jit_solution(13785978063765822721)
XLA Ops:
  0.6 1.3 select_reduce_fusion.order
  1.9 0.7 convert_element_type.9
  2.6 1.3 broadcast_in_dim.37.gain
  3.9 1.3 broadcast_in_dim.38.bias
  5.1 1.3 broadcast_in_dim.34.segrow
  6.4 0.7 convert_element_type.11
  7.1 0.6 broadcast_in_dim.36.mgate
  7.7 0.1 broadcast_in_dim.35
  7.8 0.7 broadcast_in_dim_reshape.6.hgate
  8.4 1.3 convert_element_type.10
  9.7 1.1 broadcast_in_dim_reshape.8.hcol
  10.8 1.7 copy.36.segcol
  12.5 120.4 %shard_map.291 = (bf16[1024,768]{1,0:T(8,128)(2,1)}, bf16[1024,2304]{1,0:T(8,128)(2,1)}, bf16[1024,768]{1,0:T(8,128)(2,1)}, bf16[768,1024]{1,0:T(8,128)(2,1)}, b...) custom-call(f32[2]{0:T(128)} %gates.3, ...), custom_call_target="tpu_custom_call" | custom-call | tf_op jit(solution)/shard_map/pallas_call | solution.py:709
  132.9 155.9 %shard_map.292 = (f32[1024,768]{1,0:T(8,128)}, bf16[6,8,48,384]{3,2,1,0:T(8,128)(2,1)}, f32[16,768]{1,0:T(8,128)}) custom-call(f32[2]{0:T(128)} %gates.3, s32[48]{0:T(128)} %select_reduce_fusion.order, f32[16,768]{1,0:T(8,128)} %get-tuple-element.33.small_in, f32[1,768]{1,0:T(1,128)} %broadcast_in_dim_reshape.6.hgate, ...), custom_call_target="tpu_custom_call" | custom-call | tf_op jit(solution)/shard_map/pallas_call | solution.py:1172
  288.8 2.1 maximum_subtract_fusion
  290.9 1.4 slice_reduce_fusion.1
  292.3 0.7 slice.16
  293.0 0.6 reshape.42
  293.7 0.1 reshape_squeeze.3
  293.7 0.6 reduce_sum.28
  294.4 0.0 copy-start
  294.4 2.0 copy-done
  296.4 1.5 copy-done.1
  297.8 1.2 copy-done.2
  299.0 1.2 copy-done.3
  300.2 1.2 copy-done.4
  301.3 1.2 copy-done.5
  302.5 5.2 %shard_map.293 = (f32[6,96,384]{2,1,0:T(8,128)}, f32[6,96,384]{2,1,0:T(8,128)}, f32[6,96,384]{2,1,0:T(8,128)}, f32[6,96,384]{2,1,0:T(8,128)}, bf16[6,96,384]{2,1,0:T(8,128)(2,1)}) custom-call(bf16[6,384,384]{2,1,0:T(8,128)(2,1)S(1)} %bitcast.4, f32[6,96,384]{2,1,0:T(8,128)S(1)} %copy-done.2, f32[6,96,384]{2,1,0:T(8,128)S(1)} %copy-done.3, ...), custom_call_target="tpu_custom_call" | custom-call | tf_op jit(solution)/shard_map/pallas_call | solution.py:1247
  307.7 0.0 copy-done.7
  307.7 1.1 copy.41
  308.9 1.3 copy-done.6
  310.2 1.7 copy.42
  (7 shorter events, 0.0 us)
Async XLA Ops:
  294.4 2.0 copy-start
  296.4 1.5 copy-start.1
  297.8 1.2 copy-start.2
  299.0 1.2 copy-start.3
  300.2 1.2 copy-start.4
  301.3 1.2 copy-start.5
  302.5 5.2 %copy-start.7 = (bf16[1024,768]{1,0:T(8,128)(2,1)S(1)}, bf16[1024,768]{1,0:T(8,128)(2,1)}, u32[]{:S(2)}) copy-start(bf16[1024,768]{1,0:T(8,128)(2,1)} %get-tuple-element.69) | copy-start | bytes 4718596
  307.7 2.5 copy-start.6

commit v3 on v2

--- a/solution.py
+++ b/solution.py
@@ -329,20 +329,41 @@
     return centre * inv, inv
 
 
-NPIECE = 6
+def one_row(v):
+    return jnp.concatenate([v[i : i + 1] for i in range(v.shape[0])], axis=1)
+
+
+def many_rows(v):
+    return jnp.concatenate([v[:, 128 * i : 128 * i + 128] for i in range(v.shape[1] // 128)], axis=0)
+
+
+def head_lanes(heads):
+    which = lax.broadcasted_iota(jnp.int32, (1, D), 1) // HD
+    row = jnp.zeros((1, D), F32)
+    for h in range(12):
+        row = row + jnp.where(which == h, heads[h].astype(F32), 0.0)
+    return row
+
+
+def columns_of(segs, segcol):
+    for b in range(2):
+        row = segs[b : b + 1, :].astype(F32)
+        segcol[b] = jnp.broadcast_to(row, (8, BLK)).T[:, 0:1].astype(jnp.int32)
+
+
+NPIECE = 8
 
 
 def forward_kernel(
     gates,
+    heads,
     tokens,
     cot,
-    segcol,
-    segrow,
-    hgate,
-    ugate,
-    mgate,
-    gain,
-    bias,
+    segs,
+    units,
+    hidden,
+    gain_in,
+    bias_in,
     qkv_in,
     out_in,
     up_in,
@@ -377,6 +398,9 @@
     inner,
     grads,
     outv,
+    segcol,
+    ugate,
+    vec,
     send_sem,
     recv_sem,
     loc_sem,
@@ -399,20 +423,23 @@
         pl.semaphore_signal(barrier, inc=1, device_id=peer, device_id_type=MESH)
     pl.semaphore_wait(barrier, 3)
 
+    def spot(j):
+        if j < 3:
+            return 0, 192, pl.ds(768 * j, 768)
+        if j == 3:
+            return 1, 192, slice(None)
+        return 2 + (j - 4) // 2, 768, pl.ds(384 * (j % 2), 384)
+
     def full(j, i, h=None):
-        if j < 3:
-            ref, n, cols = wq, 192, pl.ds(768 * j, 768)
-        else:
-            ref, n, cols = ((wo, 192), (wu, 768), (wd, 768))[j - 3] + (slice(None),)
+        which, n, cols = spot(j)
+        ref = (wq, wo, wu, wd)[which]
         if h is None:
             return ref.at[i, :, cols]
         return ref.at[i, pl.ds(pl.multiple_of(h * (n // 2), 16), n // 2), cols]
 
     def own(j, h=None):
-        if j < 3:
-            ref, n, cols = qkv_in, 192, pl.ds(768 * j, 768)
-        else:
-            ref, n, cols = ((out_in, 192), (up_in, 768), (down_in, 768))[j - 3] + (slice(None),)
+        which, n, cols = spot(j)
+        ref = (qkv_in, out_in, up_in, down_in)[which]
         if h is None:
             return ref.at[:, cols]
         return ref.at[pl.ds(pl.multiple_of(h * (n // 2), 16), n // 2), cols]
@@ -474,6 +501,14 @@
     for j in range(3):
         first(j)
 
+    columns_of(segs, segcol)
+    for i in range(4):
+        ugate[i] = one_row(units[6 * i : 6 * i + 6, :].astype(F32))
+    vec[0:1, :] = head_lanes(heads)
+    vec[1:2, :] = one_row(hidden[...].astype(F32))
+    vec[2:3, :] = one_row(gain_in[...])
+    vec[3:4, :] = one_row(bias_in[...])
+    hgate, mgate, gain, bias = (vec.at[i : i + 1] for i in range(4))
     tokT[...] = tokens[...].T
     tok_copy = pltpu.make_async_copy(tokT, o_tokT, out_sem.at[0])
     tok_copy.start()
@@ -485,28 +520,32 @@
         blow[rows, :] = low
         bT[:, rows] = low.T
 
+    def project(j):
+        @pl.loop(0, 2)
+        def _(r):
+            rows = pl.ds(pl.multiple_of(r * 512, 512), 512)
+            w = wq[:, :, pl.ds(768 * j, 768)].reshape(D, D)
+            joined[rows, pl.ds(768 * j, 768)] = nn(tokens[rows, :], w).astype(BF)
+
     second(0)
     second(1)
     third(0)
     second(2)
-    third(1)
-    third(2)
     for j in range(3, NPIECE):
         first(j)
-    for j in range(3):
-        finish_near(j)
-        finish_far(j)
+    third(1)
+    finish_near(0)
+    finish_far(0)
+    project(0)
+    third(2)
+    finish_near(1)
+    finish_far(1)
+    project(1)
+    finish_near(2)
+    finish_far(2)
     wq_copy = pltpu.make_async_copy(wq, o_wq, out_sem.at[1])
     wq_copy.start()
-
-    for j in range(3):
-
-        @pl.loop(0, 4)
-        def _(r, j=j):
-            rows = pl.ds(pl.multiple_of(r * 256, 256), 256)
-            w = wq[:, :, pl.ds(768 * j, 768)].reshape(D, D)
-            joined[rows, pl.ds(768 * j, 768)] = nn(tokens[rows, :], w).astype(BF)
-
+    project(2)
     joined_copy = pltpu.make_async_copy(joined, o_joined, out_sem.at[2])
     joined_copy.start()
 
@@ -523,7 +562,7 @@
         k = joined[rows, pl.ds(D + lane, 128)]
         v = joined[rows, pl.ds(2 * D + lane, 128)]
         sc = segcol[b]
-        sr = segrow[b]
+        sr = segs[pl.ds(b, 1), :]
         for qt in range(2):
             cols = slice(qt * 256, qt * 256 + 256)
             allowed = sc == sr[:, cols]
@@ -542,13 +581,23 @@
             ctxT[pl.ds(lane, 128), qrows] = total.astype(BF)
             ctx[qrows, pl.ds(lane, 128)] = total.T.astype(BF)
 
-    pl.loop(0, 3)(attend)
-    second(3)
-    pl.loop(3, 5)(attend)
-    third(3)
-    pl.loop(5, 10)(attend)
-    second(4)
-    pl.loop(10, 12)(attend)
+    plan = {
+        0: [lambda: second(3)],
+        3: [lambda: second(4), lambda: third(3)],
+        8: [lambda: second(5), lambda: third(4)],
+        11: [lambda: second(6)],
+    }
+
+    @pl.loop(0, 12)
+    def _(i):
+        attend(i)
+        for at_step, todo in plan.items():
+
+            @pl.when(i == at_step)
+            def _(todo=todo):
+                for f in todo:
+                    f()
+
     ctx_copy = pltpu.make_async_copy(ctx, o_ctx, out_sem.at[3])
     ctx_copy.start()
     ctxT_copy = pltpu.make_async_copy(ctxT, o_ctxT, out_sem.at[4])
@@ -569,20 +618,17 @@
         hlow[rows, :] = low
         hT[:, rows] = low.T
 
-    third(4)
-    second(5)
+    third(5)
 
     small[...] = jnp.zeros_like(small)
 
-    def feed(u, begin, slot):
-        if not begin:
-            pass
+    def feed(u, begin, slot, between=None):
         w_up = wu.at[u]
         w_down = wd.at[u]
 
-        @pl.loop(0, 4)
+        @pl.loop(0, 2)
         def _(r):
-            rows = pl.ds(pl.multiple_of(r * 256, 256), 256)
+            rows = pl.ds(pl.multiple_of(r * 512, 512), 512)
             pre = nn(hlow[rows, :], w_up[...])
             back = nn(blow[rows, :], w_down[...])
             active, slope = gelu_parts(pre)
@@ -601,17 +647,17 @@
                 branch[rows, :] += up_part
                 hback[rows, :] += back_part
 
+        if between is not None:
+            between()
+
         for which, (left, right) in enumerate(((hT, inner), (bT, act))):
 
-            @pl.loop(0, 8)
-            def _(t, which=which, left=left, right=right):
-                rr = pl.ds(pl.multiple_of(t * 96, 16), 96)
+            @pl.loop(0, 2)
+            def _(r, which=which, left=left, right=right):
+                rr = pl.ds(pl.multiple_of(r * SB, 128), SB)
                 g = nn(left[rr, :], right[...]).astype(BF)
                 for j in range(2):
-                    for h in range(2):
-                        grads[slot, which, t // 4, j, t % 4 * 2 + h] = g[
-                            48 * h : 48 * h + 48, 384 * j : 384 * j + 384
-                        ]
+                    grads[slot, which, r, j] = g[:, SB * j : SB * j + SB].reshape(8, 48, SB)
 
     def grad_copies(u, slot):
         found = []
@@ -626,17 +672,22 @@
                 )
         return found
 
-    finish_near(4)
-    finish_near(5)
-    feed(m, True, 0)
+    for j in range(4, NPIECE):
+        finish_near(j)
+
+    def forward_rest():
+        second(7)
+        third(6)
+
+    feed(m, True, 0, forward_rest)
     for g in grad_copies(m, 0):
         g.start()
-    third(5)
+    third(7)
     feed(ms, False, 1)
     for g in grad_copies(ms, 1):
         g.start()
-    finish_far(4)
-    finish_far(5)
+    for j in range(4, NPIECE):
+        finish_far(j)
     for g in grad_copies(m, 0):
         g.wait()
     feed(my, False, 0)
@@ -688,7 +739,7 @@
         finish_sends(j)
 
 
-def run_forward(gates, tokens, cot, segcol, segrow, hgate, ugate, mgate, gain, bias, qkv, out, up, down):
+def run_forward(*arrays):
     sds = jax.ShapeDtypeStruct
     outs = (
         sds((ROWS, D), BF),
@@ -709,7 +760,7 @@
     return pl.pallas_call(
         forward_kernel,
         out_shape=outs,
-        in_specs=[sm] + [vm] * 9 + [any_] * 4,
+        in_specs=[sm] * 2 + [vm] * 7 + [any_] * 4,
         out_specs=[any_] * 9 + [vm] * 2,
         scratch_shapes=[
             pltpu.VMEM((4, 192, 3 * D), BF),
@@ -731,6 +782,9 @@
             pltpu.VMEM((ROWS, D), BF),
             pltpu.VMEM((2, 2, 2, 2, 8, 48, SB), BF),
             pltpu.VMEM((ROWS, D), BF),
+            pltpu.VMEM((2, BLK, 1), jnp.int32),
+            pltpu.VMEM((4, 1, D), F32),
+            pltpu.VMEM((8, D), F32),
             pltpu.SemaphoreType.DMA((NPIECE, 5)),
             pltpu.SemaphoreType.DMA((NPIECE, 5)),
             pltpu.SemaphoreType.DMA((NPIECE,)),
@@ -740,22 +794,22 @@
         compiler_params=pltpu.CompilerParams(
             collective_id=1, has_side_effects=True, vmem_limit_bytes=64 << 20
         ),
-    )(gates, tokens, cot, segcol, segrow, hgate, ugate, mgate, gain, bias, qkv, out, up, down)
+    )(*arrays)
 
 
 SENT = (12, 13, 14, 15, 0, 2, 4, 6, 8, 10, 1, 3, 5, 7, 9, 11)
-GROUPS = ((0, 8), (8, 8), (16, 8), (24, 8), (32, 10), (42, 6))
+GROUPS = ((0, 8), (8, 8), (16, 8), (24, 8), (32, 4), (36, 6), (42, 6))
 FF_BLOCKS = 32
+PARTS = 3
+PER = 6 // PARTS
 
 
 def backward_kernel(
     gates,
+    heads,
     order,
     small_in,
-    hgate,
-    hcol,
-    segcol,
-    segrow,
+    segs,
     lse,
     g_in,
     joined_in,
@@ -784,18 +838,24 @@
     got2,
     got3,
     part,
+    gotz,
+    total,
     slots,
-    gotz,
     gz,
     gfull,
     sm,
     gots,
+    segcol,
+    hrow,
+    hcol,
     load_sem,
     half_sem,
     send_sem,
     recv_sem,
     z_send,
     z_recv,
+    a_send,
+    a_recv,
     f_send,
     f_recv,
     s_send,
@@ -928,6 +988,20 @@
         for copy in swap3(g):
             copy.start()
 
+    spare = 1 + c
+
+    def unit(zz):
+        return zz - (zz + 3 - spare) // 4
+
+    def swapz(g, k):
+        base, count = GROUPS[g]
+        return remote(
+            part.at[pl.ds(base, count), unit((z + k) % 4)],
+            gotz.at[k - 1, pl.ds(base, count)],
+            (z_send.at[g, k - 1], z_recv.at[g, k - 1]),
+            zpeers[k - 1],
+        )
+
     def step3(g):
         base, count = GROUPS[g]
         for copy in swap3(g):
@@ -935,26 +1009,50 @@
 
         @pl.loop(base, base + count)
         def _(i):
-            part[i] = plus(block(base)(i)[y, x], got3[i])
-
-    small_peers = [sib, ypeer, xpeer] + zpeers
+            part[i] = plus(block(base)(i)[y, x], got3[i]).reshape(3, 16, SB)
+
+        for k in (1, 2, 3):
+
+            @pl.when((z + k) % 4 != spare)
+            def _(k=k):
+                swapz(g, k).start()
+
+    def step4(g):
+        base, count = GROUPS[g]
+
+        @pl.when(z != spare)
+        def _():
+            for k in (1, 2, 3):
+                swapz(g, k).wait_recv()
+
+            @pl.loop(base, base + count)
+            def _(i):
+                value = part[i, unit(z)].astype(F32)
+                for k in range(3):
+                    value = value + gotz[k, i].astype(F32)
+                total[i] = value.astype(BF)
+
+    small_peers = [sib, ypeer, xpeer, diag] + zpeers
+    small_stage = ((0,), (1, 2, 3), (4, 5, 6))
 
     def small_copy(k):
-        return remote(sm.at[min(k, 3)], gots.at[k], (s_send.at[k], s_recv.at[k]), small_peers[k])
-
-    def small_step(k):
-        small_copy(k).wait_recv()
-        if k < 3:
-            sm[k + 1] = sm[k] + gots[k]
-            if k < 2:
-                small_copy(k + 1).start()
-            else:
-                for j in (3, 4, 5):
-                    small_copy(j).start()
+        stage = 0 if k == 0 else 1 if k < 4 else 2
+        return remote(sm.at[stage], gots.at[k], (s_send.at[k], s_recv.at[k]), small_peers[k])
+
+    def small_send(stage):
+        for k in small_stage[stage]:
+            small_copy(k).start()
+
+    def small_take(stage):
+        value = sm[stage]
+        for k in small_stage[stage]:
+            small_copy(k).wait_recv()
+            value = value + gots[k]
+        if stage < 2:
+            sm[stage + 1] = value
+            small_send(stage + 1)
         else:
-            small_copy(4).wait_recv()
-            small_copy(5).wait_recv()
-            small_out[...] = sm[3] + gots[3] + gots[4] + gots[5]
+            small_out[...] = value
 
     for g in range(4):
         swap1(g).start()
@@ -962,10 +1060,15 @@
     for copy in loads[4:]:
         copy.start()
 
+    columns_of(segs, segcol)
+    hrow[...] = head_lanes(heads)
+    hcol[...] = jnp.broadcast_to(hrow[...], (8, D)).T[:, 0:1]
+    hgate = hrow
+    sm[0] = small_in[...]
+    step1(0)
     loads[0].wait()
     loads[1].wait()
     loads[2].wait()
-    sm[0] = small_in[...]
 
     @pl.loop(0, 4)
     def _(r):
@@ -976,27 +1079,23 @@
         sm[0, 9:10, :] += colsum(ctx[rows, :].astype(F32) * grad.astype(F32))
         cgrad[rows, :] = grad * hgate[...].astype(BF)
 
-    small_copy(0).start()
+    small_send(0)
+    step1(1)
     loads[3].wait()
 
     def weight_tiles(left, right, lane, rowgate, places):
-        @pl.loop(0, 8)
-        def _(t):
-            rr = pl.ds(pl.multiple_of(t * 96, 16), 96)
+        @pl.loop(0, 2)
+        def _(r):
+            rr = pl.ds(pl.multiple_of(r * SB, 128), SB)
             g = nn(left[rr, :], right[:, pl.ds(lane, SB)])
             if rowgate is not None:
                 g = g * rowgate[rr, :]
-            g = g.astype(BF)
-            to = places[0] + (t // 4) * (places[1] - places[0])
-            u = t % 4
-            for h in range(2):
-                ga[to, u // 2, u % 2, h] = g[48 * h : 48 * h + 48]
+            ga[places[0] + r * (places[1] - places[0])] = g.astype(BF).reshape(2, 2, 2, 48, SB)
 
     for j in range(2):
         weight_tiles(ctxT, outb, SB * j, hcol, (SENT.index(12 + j), SENT.index(14 + j)))
 
-    step1(0)
-    step1(1)
+    swap1(4).start()
     step1(2)
     step1(3)
     loads[4].wait()
@@ -1016,7 +1115,7 @@
         v = joined[rows, pl.ds(2 * D + lane, 128)]
         do = cgrad[rows, pl.ds(lane, 128)]
         sc = segcol[b]
-        sr = segrow[b]
+        sr = segs[pl.ds(b, 1), :]
         dv = None
         dk = None
         for qt in range(2):
@@ -1049,18 +1148,19 @@
     def middle():
         loads[5].wait()
         qkv_tiles(0)
-        swap1(4).start()
+        swap1(5).start()
 
     plan = {
-        0: [lambda: small_step(0)],
-        1: [lambda: step2(0), lambda: small_step(1)],
-        2: [lambda: small_step(2)],
-        3: [lambda: step2(1), lambda: small_step(3)],
-        5: [lambda: step2(2), middle],
-        6: [lambda: step1(4), lambda: step3(0)],
-        7: [lambda: step2(3), lambda: step3(1)],
-        8: [lambda: step3(2)],
-        10: [lambda: step2(4), lambda: step3(3)],
+        0: [lambda: small_take(0)],
+        1: [lambda: step1(4)],
+        2: [lambda: step2(0)],
+        4: [lambda: step2(1)],
+        5: [middle],
+        6: [lambda: step1(5), lambda: step2(2)],
+        7: [lambda: small_take(1)],
+        8: [lambda: step2(3)],
+        9: [lambda: step3(0), lambda: step2(4)],
+        11: [lambda: small_take(2), lambda: step3(1)],
     }
 
     @pl.loop(0, 12)
@@ -1074,86 +1174,115 @@
                     f()
 
     qkv_tiles(1)
-    swap1(5).start()
+    swap1(6).start()
     loads[6].wait()
 
     def input_rows(lo, hi):
         @pl.loop(lo, hi)
         def _(r):
-            rows = pl.ds(pl.multiple_of(r * 128, 128), 128)
+            rows = pl.ds(pl.multiple_of(r * 256, 256), 256)
             igrad[rows, :] = sgrad[rows, :] + nt(joined[rows, :], wq[...].reshape(D, 3 * D))
 
-    input_rows(0, 2)
-    step1(5)
+    step3(2)
+    step2(5)
+    step1(6)
+    input_rows(0, 1)
+    step4(0)
+    step3(3)
+    input_rows(1, 2)
+    step4(1)
     step3(4)
-    input_rows(2, 6)
-    step2(5)
-    input_rows(6, 8)
+    input_rows(2, 3)
+    step4(2)
+    step3(5)
+    input_rows(3, 4)
     igrad_copy = pltpu.make_async_copy(igrad, o_igrad, out_sem.at[0])
     igrad_copy.start()
-    step3(5)
-
-    @pl.loop(0, 48)
-    def _(s):
-        slots[s] = part[order[s]]
-
-    z_copies = []
-    for k in (1, 2, 3):
-        other = (z + k) % 4
-        z_copies.append(
-            remote(
-                slots.at[pl.ds(12 * other, 12)],
-                gotz.at[k - 1],
-                (z_send.at[k - 1], z_recv.at[k - 1]),
-                zpeers[k - 1],
-            )
+    step2(6)
+    step4(3)
+    step4(4)
+    step4(5)
+    step3(6)
+    step4(6)
+
+    def deal(n, k, to, u):
+        return remote(
+            slots.at[to, :, n],
+            gz.at[:, n, :, u],
+            (a_send.at[n, k - 1], a_recv.at[n, k - 1]),
+            zpeers[k - 1],
         )
-    for copy in z_copies:
-        copy.start()
-    for copy in z_copies:
-        copy.wait_recv()
-
-    @pl.loop(0, 12)
-    def _(s):
-        total = slots[12 * z + s].astype(F32)
+
+    @pl.when(z != spare)
+    def _():
+        @pl.loop(0, 48)
+        def _(s):
+            slots[s // 12, s // 6 % 2, s // PER % PARTS, s % PER] = total[order[s]]
+
+        for n in range(PARTS):
+            for k in (1, 2, 3):
+                deal(n, k, (z + k) % 4, unit(z)).start()
+            gz[:, n, :, unit(z)] = slots[z, :, n]
+
+    def piece(n, cc, yy, xx):
+        return gfull.at[n, :, 4 * cc + 2 * yy + xx]
+
+    others = ((y, 1 - x), (1 - y, x), (1 - y, 1 - x))
+
+    def near(n, k):
+        src = gz.at[1 - x if k in (0, 2) else x, n]
+        sems = (f_send.at[n, k], f_recv.at[n, k])
+        return remote(src, piece(n, c, y, x), sems, (xpeer, ypeer, diag, sib)[k])
+
+    def onward(n, k):
+        yy, xx = others[k]
+        to = piece(n, c, yy, xx)
+        return remote(to, to, (f_send.at[n, 4 + k], f_recv.at[n, 4 + k]), sib)
+
+    def pass_on(n):
         for k in range(3):
-            total = total + gotz[k, s].astype(F32)
-        gz[s] = total.astype(BF)
-
-    def piece(cc, yy, xx):
-        return gfull.at[:, 4 * cc + 2 * yy + xx]
-
-    here = gz.at[pl.ds(6 * x, 6)]
-    there = gz.at[pl.ds(6 * (1 - x), 6)]
-
-    def fsem(k):
-        return f_send.at[k], f_recv.at[k]
-
-    near = [
-        remote(there, piece(c, y, x), fsem(0), xpeer),
-        remote(here, piece(c, y, x), fsem(1), ypeer),
-        remote(there, piece(c, y, x), fsem(2), diag),
-        remote(here, piece(c, y, x), fsem(3), sib),
-    ]
-    for copy in near:
-        copy.start()
-    own_copy = pltpu.make_async_copy(here, piece(c, y, x), out_sem.at[1])
-    own_copy.start()
-    onward = []
-    for k, (yy, xx) in enumerate(((y, 1 - x), (1 - y, x), (1 - y, 1 - x))):
-        near[k].wait_recv()
-        copy = remote(piece(c, yy, xx), piece(c, yy, xx), fsem(4 + k), sib)
-        copy.start()
-        onward.append(copy)
-    near[3].wait_recv()
-    for copy in onward:
-        copy.wait_recv()
-    own_copy.wait()
+            near(n, k).wait_recv()
+            onward(n, k).start()
+
+    for n in range(PARTS):
+        for k in (1, 2, 3):
+            sender = (z + 4 - k) % 4
+
+            @pl.when(sender != spare)
+            def _(n=n, k=k, sender=sender):
+                deal(n, k, z, unit(sender)).wait_recv()
+
+        for k in range(4):
+            near(n, k).start()
+        gfull[n, :, 4 * c + 2 * y + x] = gz[x, n]
+        if n:
+            pass_on(n - 1)
+    pass_on(PARTS - 1)
+    for n in range(PARTS):
+        near(n, 3).wait_recv()
+        for k in range(3):
+            onward(n, k).wait_recv()
     full_copy = pltpu.make_async_copy(gfull, o_full, out_sem.at[2])
     full_copy.start()
-    for copy in near + onward + z_copies:
-        copy.wait_send()
-    for k in range(6):
+    for n in range(PARTS):
+        for k in range(4):
+            near(n, k).wait_send()
+        for k in range(3):
+            onward(n, k).wait_send()
+
+        @pl.when(z != spare)
+        def _(n=n):
+            for k in (1, 2, 3):
+                deal(n, k, (z + k) % 4, unit(z)).wait_send()
+
+    for g in range(len(GROUPS)):
+        for k in (1, 2, 3):
+
+            @pl.when((z + k) % 4 != spare)
+            def _(g=g, k=k):
+                swapz(g, k).wait_send()
+
+    for k in range(7):
         small_copy(k).wait_send()
     for g in range(len(GROUPS)):
         for copy in (swap1(g),) + swap2(g) + swap3(g):
@@ -1162,9 +1291,9 @@
     full_copy.wait()
 
 
-def run_backward(gates, order, small, hgate, hcol, segcol, segrow, lse, *arrays):
+def run_backward(*arrays):
     sds = jax.ShapeDtypeStruct
-    outs = (sds((ROWS, D), F32), sds((6, 8, 48, SB), BF), sds((16, D), F32))
+    outs = (sds((ROWS, D), F32), sds((PARTS, PER, 8, 3, 16, SB), BF), sds((16, D), F32))
     any_ = pl.BlockSpec(memory_space=pl.ANY)
     vm = pl.BlockSpec(memory_space=pltpu.VMEM)
     sm = pl.BlockSpec(memory_space=pltpu.SMEM)
@@ -1172,7 +1301,7 @@
     return pl.pallas_call(
         backward_kernel,
         out_shape=outs,
-        in_specs=[sm] * 2 + [vm] * 6 + [any_] * 8,
+        in_specs=[sm] * 3 + [vm] * 3 + [any_] * 8,
         out_specs=[any_] * 2 + [vm],
         scratch_shapes=[
             pltpu.VMEM((ROWS, 3 * D), BF),
@@ -1190,29 +1319,35 @@
             pltpu.VMEM((48, 2, 2, 48, SB), BF),
             pltpu.VMEM((48, 2, 48, SB), BF),
             pltpu.VMEM((48, 48, SB), BF),
-            pltpu.VMEM((48, 48, SB), BF),
-            pltpu.VMEM((48, 48, SB), BF),
-            pltpu.VMEM((3, 12, 48, SB), BF),
-            pltpu.VMEM((12, 48, SB), BF),
-            pltpu.VMEM((6, 8, 48, SB), BF),
-            pltpu.VMEM((4, 16, D), F32),
-            pltpu.VMEM((6, 16, D), F32),
+            pltpu.VMEM((48, 3, 16, SB), BF),
+            pltpu.VMEM((3, 48, 16, SB), BF),
+            pltpu.VMEM((48, 16, SB), BF),
+            pltpu.VMEM((4, 2, PARTS, PER, 16, SB), BF),
+            pltpu.VMEM((2, PARTS, PER, 3, 16, SB), BF),
+            pltpu.VMEM((PARTS, PER, 8, 3, 16, SB), BF),
+            pltpu.VMEM((3, 16, D), F32),
+            pltpu.VMEM((7, 16, D), F32),
+            pltpu.VMEM((2, BLK, 1), jnp.int32),
+            pltpu.VMEM((1, D), F32),
+            pltpu.VMEM((D, 1), F32),
             dma((7,)),
             dma((4,)),
-            dma((6, 5)),
-            dma((6, 5)),
-            dma((3,)),
-            dma((3,)),
+            dma((7, 5)),
+            dma((7, 5)),
+            dma((7, 3)),
+            dma((7, 3)),
+            dma((PARTS, 3)),
+            dma((PARTS, 3)),
+            dma((PARTS, 7)),
+            dma((PARTS, 7)),
             dma((7,)),
             dma((7,)),
-            dma((6,)),
-            dma((6,)),
             dma((3,)),
         ],
         compiler_params=pltpu.CompilerParams(
             collective_id=2, has_side_effects=True, vmem_limit_bytes=64 << 20
         ),
-    )(gates, order, small, hgate, hcol, segcol, segrow, lse, *arrays)
+    )(*arrays)
 
 
 def split(value):
@@ -1221,8 +1356,66 @@
 
 
 def update_kernel(
-    full, master, left_stats, right_stats, left_root, right_root, o_grad, o_left, o_right, o_new, o_copy, turned
+    small,
+    gain,
+    bias,
+    full,
+    master,
+    left_stats,
+    right_stats,
+    left_root,
+    right_root,
+    out_in,
+    igrad_in,
+    o_grad,
+    o_left,
+    o_right,
+    o_new,
+    o_copy,
+    o_unit,
+    o_hidden,
+    o_head,
+    o_layer,
+    o_norm,
+    o_norm_new,
+    o_out,
+    o_igrad,
+    turned,
+    stage_out,
+    stage_igrad,
+    sem,
 ):
+    slot = pl.program_id(0)
+    moves_in = (
+        pltpu.make_async_copy(out_in, stage_out, sem.at[0]),
+        pltpu.make_async_copy(igrad_in, stage_igrad, sem.at[1]),
+    )
+    moves = (
+        pltpu.make_async_copy(stage_out, o_out, sem.at[2]),
+        pltpu.make_async_copy(stage_igrad, o_igrad, sem.at[3]),
+    )
+
+    @pl.when(slot == 0)
+    def _():
+        for move in moves_in:
+            move.start()
+        for i in range(4):
+            o_unit[6 * i : 6 * i + 6, :] = many_rows(small[i : i + 1, :])
+        o_hidden[...] = many_rows(small[6:7, :])
+        o_norm[...] = small[4:6, :]
+        rate = 0.2 / math.sqrt(ROWS * 32)
+        o_norm_new[0:1, :] = one_row(gain[...]) - rate * small[4:5, :]
+        o_norm_new[1:2, :] = one_row(bias[...]) - rate * small[5:6, :]
+        lane = lax.broadcasted_iota(jnp.int32, (16, D), 1) // HD
+        row = lax.broadcasted_iota(jnp.int32, (16, D), 0)
+        by_head = jnp.sum(jnp.where(lane == row, small[9:10, :], 0.0), axis=1, keepdims=True)
+        square = lax.broadcasted_iota(jnp.int32, (16, 128), 1)
+        diagonal = square == lax.broadcasted_iota(jnp.int32, (16, 128), 0)
+        o_head[...] = jnp.sum(jnp.where(diagonal, by_head, 0.0), axis=0, keepdims=True)[:, :12]
+        pair = jnp.sum(small[7:9, :], axis=1, keepdims=True)
+        first = lax.broadcasted_iota(jnp.int32, (1, 2), 1) == 0
+        o_layer[...] = jnp.where(first, pair[0:1], pair[1:2])
+
     start = pl.multiple_of(lax.axis_index("mp") * 96, 16)
     own = full[0, pl.ds(start, 96), :]
     whole = full[0]
@@ -1239,20 +1432,54 @@
     o_new[0] = new
     o_copy[0] = new.astype(BF)
 
-
-def run_update(full, master, left_stats, right_stats, left_root, right_root):
+    @pl.when(slot == 2)
+    def _():
+        for first, then in zip(moves_in, moves):
+            first.wait()
+            then.start()
+
+    @pl.when(slot == 5)
+    def _():
+        for move in moves:
+            move.wait()
+
+
+def run_update(*arrays):
     sds = jax.ShapeDtypeStruct
     whole = pl.BlockSpec((1, SB, SB), lambda s: (s, 0, 0))
     rows = pl.BlockSpec((1, 96, SB), lambda s: (s, 0, 0))
+    any_ = pl.BlockSpec(memory_space=pl.ANY)
+
+    def const(*shape):
+        return pl.BlockSpec(shape, lambda s: (0, 0))
+
+    flat = const(6, 128)
     return pl.pallas_call(
         update_kernel,
         grid=(6,),
-        out_shape=(sds((6, 96, SB), F32),) * 4 + (sds((6, 96, SB), BF),),
-        in_specs=[whole] + [rows] * 4 + [whole],
-        out_specs=[rows] * 5,
-        scratch_shapes=[pltpu.VMEM((SB, SB), BF)],
-        compiler_params=pltpu.CompilerParams(vmem_limit_bytes=32 << 20),
-    )(full, master, left_stats, right_stats, left_root, right_root)
+        out_shape=(sds((6, 96, SB), F32),) * 4
+        + (
+            sds((6, 96, SB), BF),
+            sds((24, 128), F32),
+            sds((6, 128), F32),
+            sds((1, 12), F32),
+            sds((1, 2), F32),
+            sds((2, D), F32),
+            sds((2, D), F32),
+            sds((ROWS, D), BF),
+            sds((ROWS, D), F32),
+        ),
+        in_specs=[const(16, D), flat, flat, whole] + [rows] * 4 + [whole] + [any_] * 2,
+        out_specs=[rows] * 5
+        + [const(24, 128), flat, const(1, 12), const(1, 2), const(2, D), const(2, D), any_, any_],
+        scratch_shapes=[
+            pltpu.VMEM((SB, SB), BF),
+            pltpu.VMEM((ROWS, D), BF),
+            pltpu.VMEM((ROWS, D), F32),
+            pltpu.SemaphoreType.DMA((4,)),
+        ],
+        compiler_params=pltpu.CompilerParams(vmem_limit_bytes=64 << 20),
+    )(*arrays)
 
 
 PLACE = tuple(FF_BLOCKS + SENT.index(b) for b in range(16)) + tuple(range(32))
@@ -1279,23 +1506,18 @@
     left_root,
     right_root,
 ):
-    segcol = segments[:, :, None]
-    segrow = segments[:, None, :]
-    head_lanes = jnp.repeat(head_mask.astype(F32), HD)
-    hgate = head_lanes[None]
-    ugate = unit_mask.astype(F32).reshape(4, 1, D)
-    mgate = hidden_mask.astype(F32)[None]
+    gain = norm_gain.reshape(6, 128)
+    bias = norm_bias.reshape(6, 128)
     (output, joined, ctx, ctxT, tokT, summed_grad, ff_grad, wq, wo, lse, small) = run_forward(
         layer_gates,
+        head_mask,
         tokens,
         cotangent,
-        segcol,
-        segrow,
-        hgate,
-        ugate,
-        mgate,
-        norm_gain[None],
-        norm_bias[None],
+        segments,
+        unit_mask.reshape(24, 128),
+        hidden_mask.reshape(6, 128),
+        gain,
+        bias,
         qkv_weight,
         out_weight,
         up_weight,
@@ -1306,12 +1528,10 @@
     )
     input_grad, full, small = run_backward(
         layer_gates,
+        head_mask,
         slot_order,
         small,
-        hgate,
-        head_lanes[:, None],
-        segcol,
-        segrow,
+        segments,
         lse,
         ff_grad.reshape(32, 2, 2, 2, 48, SB),
         joined,
@@ -1322,22 +1542,40 @@
         wq,
         wo,
     )
-    owned, left_new, right_new, weight_new, weight_copy = run_update(
-        full.reshape(6, SB, SB), master, left_stats, right_stats, left_root, right_root
-    )
-    unit_grad = small[:4].reshape(-1)
-    norm_grad = small[4:6]
-    mask_grad = small[6]
-    layer_grad = jnp.sum(small[7:9], axis=1)
-    head_grad = jnp.sum(small[9].reshape(12, HD), axis=1)
-    norm_new = jnp.stack([norm_gain, norm_bias]) - 0.2 / math.sqrt(ROWS * 32) * norm_grad
+    (
+        owned,
+        left_new,
+        right_new,
+        weight_new,
+        weight_copy,
+        unit_grad,
+        hidden_grad,
+        head_grad,
+        layer_grad,
+        norm_grad,
+        norm_new,
+        output,
+        input_grad,
+    ) = run_update(
+        small,
+        gain,
+        bias,
+        full.reshape(6, SB, SB),
+        master,
+        left_stats,
+        right_stats,
+        left_root,
+        right_root,
+        output,
+        input_grad,
+    )
     return (
         output,
         input_grad,
-        head_grad,
-        unit_grad,
-        mask_grad,
-        layer_grad,
+        head_grad.reshape(12),
+        unit_grad.reshape(FF),
+        hidden_grad.reshape(D),
+        layer_grad.reshape(2),
         norm_grad,
         norm_new,
         owned,

time: 313 us -> 214 us (0.68)
  Pallas kernels: 281 us -> 210 us
  local copies, waits for them, and re-layouts: 23 us -> 0 us
  other arithmetic: 6.7 us -> 1.3 us
    pallas_call x2, Pallas kernels: 276 us -> 199 us  [the longest x1 106 us: run_backward(): pl.pallas_call(backward_kernel, out_shape=outs, in_specs=[sm] * 3 + [vm]...]
    unnamed x18 -> x0, local copies, waits for them, and re-layouts: 12.3 us -> none
    broadcast_in_dim x6 -> x0, local copies, waits for them, and re-layouts: 6.17 us -> none  [the longest x1 1.71 us: fast_body(): segcol = segments[:, :, None]]
    pallas_call x1, Pallas kernels: 5.21 us -> 11.1 us  [run_update(): pl.pallas_call(update_kernel, grid=(6,), out_shape=(sds((6, 96, SB), F32)...]
where the time goes in v3:
time: 214 us; the launch traced here: 212 us
  Pallas kernels  210 us (98%)
    pallas_call x1, Pallas kernels, run_backward(): pl.pallas_call(backward_kernel, out_shape=outs, in_specs=[sm] * 3 + [vm]...  106 us
    pallas_call x1, Pallas kernels, run_forward(): pl.pallas_call(forward_kernel, out_shape=outs, in_specs=[sm] * 2 + [vm] *...  92.8 us
    pallas_call x1, Pallas kernels, run_update(): pl.pallas_call(update_kernel, grid=(6,), out_shape=(sds((6, 96, SB), F32)...  11.1 us

profile of v3, /device:TPU:9, one launch (start us, length us, event | category | flops | bytes accessed | tf_op | source)
XLA Modules:
  0.0 212.2 jit_solution(16103797094558424312)
XLA Ops:
  0.6 1.3 select_reduce_fusion.order
  1.9 92.8 %shard_map.291 = (bf16[1024,768]{1,0:T(8,128)(2,1)}, bf16[1024,2304]{1,0:T(8,128)(2,1)}, bf16[1024,768]{1,0:T(8,128)(2,1)}, bf16[768,1024]{1,0:T(8,128)(2,1)}, b...) custom-call(f32[2]{0:T(128)} %gates.3, s32[12]{0:T(128)} %heads.3, ...), custom_call_target="tpu_custom_call" | custom-call | tf_op jit(solution)/shard_map/pallas_call | solution.py:760
  94.7 106.2 %shard_map.292 = (f32[1024,768]{1,0:T(8,128)}, bf16[3,2,8,3,16,384]{5,4,3,2,1,0:T(8,128)(2,1)}, f32[16,768]{1,0:T(8,128)}) custom-call(f32[2]{0:T(128)} %gates.3, s32[12]{0:T(128)} %heads.3, s32[48]{0:T(128)} %select_reduce_fusion.order, f32[16,768]{1,0:T(8,128)} %get-tuple-element.40.small_in, s32[2,512]{1,0:T(2,128)} %segs.3, ...), custom_call_target="tpu_custom_call" | custom-call | tf_op jit(solution)/shard_map/pallas_call | solution.py:1301
  200.9 11.1 %shard_map.293 = (f32[6,96,384]{2,1,0:T(8,128)}, f32[6,96,384]{2,1,0:T(8,128)}, f32[6,96,384]{2,1,0:T(8,128)}, f32[6,96,384]{2,1,0:T(8,128)}, bf16[6,96,384]{2,1...) custom-call(f32[16,768]{1,0:T(8,128)} %get-tuple-element.50.small, ...), custom_call_target="tpu_custom_call" | custom-call | tf_op jit(solution)/shard_map/pallas_call | solution.py:1457
